TPU v7x, 512 devices: a whole 4x4x16 slice. The times are simulated.
512 devices in a mesh: space: 32 (over z, core), mode: 16 (over y, x).
Axes of the slice: x: 4, y: 4, z: 16, core: 2. Of those that a mesh axis runs over, the one named last changes fastest.
Arguments:
- basis: float32 [65536, 1024], P('space', 'mode'), may hold values from -0.0234375 to 0.0234375
- snapshots: float32 [65536, 64], P('space'), may hold values from -6 to 6
- rotation: float32 [1088, 1024], replicated, may hold values from -0.1875 to 0.1875
Outputs:
- scaled_basis: float32 [65536, 1024], P('space', 'mode')
- factor: float32 [64, 64], replicated
All inputs are finite; a program needn't handle non-finite values.
Results may differ from a plain program's by a relative error of at most 0.00007.
Values sent between devices are 32-bit elements; how exact they have to be, the bound alone decides.
No kernel may reach another device: no remote copies, remote signals or barrier semaphores. Data moves between devices by JAX's collectives and lax.ppermute only.
A program may use at most 64 MiB of HBM per device.

v0:
```python
import jax
import jax.numpy as jnp
from jax import lax
from jax.sharding import PartitionSpec as P


def local(basis, snapshots, rotation):
    high = lax.Precision.HIGHEST
    row_count = basis.shape[0]
    local_modes = basis.shape[1]
    modes_all = rotation.shape[1]
    place = lax.axis_index("mode")
    scale = jnp.sqrt(jnp.float32(row_count * lax.axis_size("space")))
    coeffs = lax.psum(jnp.dot(basis.T, snapshots, precision=high), "space")
    partial_back = jnp.dot(basis, coeffs, precision=high)
    resid = snapshots - lax.psum(partial_back, "mode")
    gram = lax.psum(jnp.dot(resid.T, resid, precision=high), "space")
    lower = jnp.linalg.cholesky(gram)
    ortho = lax.linalg.triangular_solve(lower, resid, left_side=False, lower=True, transpose_a=True)
    own_columns = lax.dynamic_slice_in_dim(rotation, place * local_modes, local_modes, 1)
    upper_cols = own_columns[:modes_all]
    lower_cols = own_columns[modes_all:]
    rotated = jnp.dot(lax.all_gather(basis, "mode", axis=1, tiled=True), upper_cols, precision=high)
    updated = rotated + jnp.dot(ortho, lower_cols, precision=high)
    return (updated * scale, lower / scale)


def solution(mesh):
    placed = (P("space", "mode"), P("space", None), P())
    return jax.shard_map(
        local, mesh=mesh, in_specs=placed, out_specs=(P("space", "mode"), P()), check_vma=False
    )
```

profile of v0, /device:TPU:1, one launch (start us, length us, event | category | flops | bytes accessed | tf_op | source)
XLA Modules:
  0.0 349.1 jit_solution(13808327447649630697)
XLA Ops:
  7.2 0.0 all-reduce.2.cloned.1.call-start
  7.2 1.8 fusion.8
  9.0 96.9 %psum.21 = f32[64,64]{1,0:T(8,128)S(1)} all-reduce(f32[64,64]{1,0:T(8,128)S(1)} %fusion.8), channel_id=1, replica_groups=mesh['space'=32,'mode'=16] {'space'}, use_global_device_ids=true, to_apply=%region_0.0 | all-reduce | flops 4096 | bytes 32768 | tf_op jit(solution)/shard_map/psum | solution.py:14
  105.9 2.5 convolution_bitcast_fusion.1
  108.3 0.0 all-reduce.2.cloned.1.call-update
  108.3 0.0 all-gather.2.cloned.1.call-start
  108.4 0.7 all-gather.2.cloned.1.call-update
  109.1 112.5 %all-reduce.2.cloned.1.call-done = f32[2048,64]{0,1:T(8,128)} async-done(((f32[2048,64]{0,1:T(8,128)}), f32[2048,64]{0,1:T(8,128)}) %all-reduce.2.cloned.1.call-update) | async-done | bytes 524304 | tf_op jit(solution)/shard_map/psum | solution.py:16
  221.6 1.3 sub.3
  222.8 0.6 fusion.9
  223.4 93.4 %psum.23 = f32[64,64]{0,1:T(8,128)S(1)} all-reduce(f32[64,64]{0,1:T(8,128)S(1)} %fusion.9), channel_id=1, replica_groups=mesh['space'=32,'mode'=16] {'space'}, use_global_device_ids=true, to_apply=%region_2.0 | all-reduce | flops 4096 | bytes 32768 | tf_op jit(solution)/shard_map/psum | solution.py:17
  316.8 0.1 copy.6
  316.9 5.8 %cholesky.16 = f32[64,64]{1,0:T(8,128)S(1)} custom-call(f32[64,64]{1,0:T(8,128)S(1)} %fusion.5), custom_call_target="Cholesky" | custom-call | tf_op jit(solution)/shard_map/jit(cholesky)/cholesky | solution.py:18
  322.8 0.6 compare_reduce_fusion
  323.4 1.3 fusion.6
  324.7 4.9 %custom-call.6 = f32[1,64,64]{1,2,0:T(8,128)S(1)} custom-call(f32[1,64,64]{2,1,0:T(8,128)S(1)} %get-tuple-element.3), custom_call_target="InvertDiagBlocksLowerTriangular" | custom-call | tf_op jit(solution)/shard_map/triangular_solve | solution.py:19
  329.6 1.8 fusion.3
  331.4 0.0 all-gather.2.cloned.1.call-done
  331.5 7.9 %convolution_bitcast_fusion = f32[2048,64]{0,1:T(8,128)S(1)} fusion(f32[2048,1024]{0,1:T(8,128)} %all-gather.2.cloned.1.call-done, f32[1088,1024]{1,0:T(8,128)} %param.5, s32[]{:T(128)S(6)} %select_n.7), kind=kOutput, calls=%fused_computation.1 | convolution fusion | flops 1610612736 | bytes 9437188 | tf_op jit(solution)/shard_map/dot_general | solution.py:23
  339.3 2.9 fusion
  (2 shorter events, 0.0 us)
Async XLA Ops:
  7.2 214.4 %all-reduce.2.cloned.1.call-start = ((), (), s32[]{:S(2)}) async-start(), calls=%async_computation.1 | async-start | bytes 1048576 | tf_op jit(solution)/shard_map/psum | solution.py:16
  108.3 223.1 %all-gather.2.cloned.1.call-start = ((), (), s32[]{:S(2)}) async-start(), calls=%async_computation | async-start | bytes 8912896 | tf_op jit(solution)/shard_map/all_gather | solution.py:23
Sparse Core Ops, SparseCore 0:
  108.5 113.0 all-reduce.1
  225.0 86.8 all-gather.1
where the time goes:
time: 350 us; the launch traced here: 349 us
  blocking collectives  190 us (54%)
  waiting for transfers between devices  113 us (32%)
  matrix products  17.4 us (5%)
  between operations  14.1 us (4%)
  other arithmetic  13.9 us (4%)
    psum x1, waiting for transfers between devices, local(): resid = snapshots - lax.psum(partial_back, 'mode')  112 us
    psum x1, blocking collectives, local(): coeffs = lax.psum(jnp.dot(basis.T, snapshots, precision=high), 'space')  96.9 us
    psum x1, blocking collectives, local(): gram = lax.psum(jnp.dot(resid.T, resid, precision=high), 'space')  93.4 us
    dot_general x1, matrix products, local(): jnp.dot(lax.all_gather(basis, 'mode', axis=1, tiled=True), upper_cols, pr...  7.87 us
  transfers between devices with their start and end apart: 2, of which 1 were waited for; matrix products, arithmetic and copies ran while one was open for 5% of the time, Pallas kernels for 0%

commit v1 on v0

v1 whole, which is shorter than its diff:
```python
import jax
import jax.numpy as jnp
from jax import lax
from jax.sharding import Mesh, PartitionSpec as P

HIGH = lax.Precision.HIGHEST
Z = "z"
CORE = "core"
MODE = ("y", "x")


def spread(block, axes, count):
    return lax.all_to_all(
        jnp.broadcast_to(block[None], (count,) + block.shape), axes, 0, 0, tiled=True
    )


def dot(a, b, left, right):
    return lax.dot_general(a, b, (((left,), (right,)), ((), ())), precision=HIGH)


def local(basis, snapshots, rotation):
    depth = lax.axis_size(Z)
    modes = lax.axis_size("y") * lax.axis_size("x")
    rows, width = basis.shape
    count = snapshots.shape[1]
    part = rows // modes
    total = rotation.shape[1]
    place = lax.axis_index(MODE)
    scale = jnp.sqrt(jnp.float32(rows * depth * 2))
    bt, st = basis.T, snapshots.T
    own = lax.all_to_all(bt.reshape(width, modes, part), MODE, 1, 0, tiled=False)
    own = own.reshape(total, part)
    coeffs = dot(bt, st, 1, 1)
    half = lax.all_to_all(coeffs.reshape(2, width // 2, count), CORE, 0, 0, tiled=True)
    half = spread(half.sum(0), Z, depth).sum(0)
    coeffs_all = spread(half, MODE + (CORE,), modes * 2).reshape(total, count)
    st_own = lax.dynamic_slice_in_dim(st, place * part, part, 1)
    resid = st_own - dot(coeffs_all, own, 0, 0)
    gram = dot(resid, resid, 1, 1)
    pieces = jnp.broadcast_to(
        gram.reshape(2, 1, count // 2, count), (2, modes, count // 2, count)
    ).reshape(2 * modes, count // 2, count)
    pieces = lax.all_to_all(pieces, (CORE,) + MODE, 0, 0, tiled=True).sum(0)
    pieces = spread(pieces, Z, depth).sum(0)
    gram = lax.all_gather(pieces, CORE, axis=0, tiled=True)
    lower = jnp.linalg.cholesky(gram)
    columns = lax.dynamic_slice_in_dim(rotation, place * width, width, 1)
    weights = lax.linalg.triangular_solve(
        lower, columns[total:], left_side=True, lower=True, transpose_a=True
    )
    rotated = dot(rotation[:total], own, 0, 0)
    rotated = lax.all_to_all(rotated.reshape(modes, width, part), MODE, 0, 1, tiled=False)
    rotated = rotated.reshape(width, rows)
    resid_all = lax.all_to_all(
        jnp.broadcast_to(resid[None], (modes, count, part)), MODE, 0, 1, tiled=False
    ).reshape(count, rows)
    updated = rotated + dot(weights, resid_all, 0, 0)
    return ((updated * scale).T, lower / scale)


def solution(mesh):
    y, x = 4, 4
    split = Mesh(mesh.devices.reshape(-1, 2, y, x), ("z", "core", "y", "x"))
    space, mode = ("z", "core"), ("y", "x")
    placed = (P(space, mode), P(space, None), P())
    return jax.shard_map(
        local, mesh=split, in_specs=placed, out_specs=(P(space, mode), P()), check_vma=False
    )
```

time: 350 us -> 157 us (0.45)
  blocking collectives: 190 us -> 28.9 us
  waiting for transfers between devices: 113 us -> 38.9 us
  starting transfers between devices: 0.08 us -> 38.7 us
  local copies, waits for them, and re-layouts: 0.07 us -> 18.2 us
  between operations: 14.1 us -> 0.87 us
  matrix products: 17.4 us -> 12.8 us
  other arithmetic: 13.9 us -> 17.9 us
    psum x2 -> x0, blocking collectives: 190 us -> none  [the longest x1 96.9 us: local(): coeffs = lax.psum(jnp.dot(basis.T, snapshots, precision=high), 'space')]
    psum x1 -> x0, waiting for transfers between devices: 112 us -> none  [local(): resid = snapshots - lax.psum(partial_back, 'mode')]
    all_to_all x0 -> x6, waiting for transfers between devices: none -> 38.9 us  [the longest x3 23.9 us: spread(): lax.all_to_all(jnp.broadcast_to(block[None], (count,) + block.shape), axe...]
    all_to_all x0 -> x6, starting transfers between devices: none -> 38.7 us  [the longest x3 24.2 us: spread(): lax.all_to_all(jnp.broadcast_to(block[None], (count,) + block.shape), axe...]
    all_to_all x0 -> x2, blocking collectives: none -> 23.3 us  [the longest x1 13 us: local(): pieces = lax.all_to_all(pieces, (CORE,) + MODE, 0, 0, tiled=True).sum(0)]
    dot_general x0 -> x2, local copies, waits for them, and re-layouts: none -> 10.1 us  [dot(): lax.dot_general(a, b, (((left,), (right,)), ((), ())), precision=HIGH)]
    all_gather x0 -> x1, blocking collectives: none -> 5.64 us  [local(): gram = lax.all_gather(pieces, CORE, axis=0, tiled=True)]
    all_to_all x0 -> x5, other arithmetic: none -> 5.11 us  [the longest x3 3.16 us: spread(): lax.all_to_all(jnp.broadcast_to(block[None], (count,) + block.shape), axe...]
  transfers between devices with their start and end apart: 2 -> 6, of which waited for: 1 -> 5; matrix products, arithmetic and copies ran while one was open for 5% -> 18% of each run, Pallas kernels for 0% -> 0%
where the time goes in v1:
time: 157 us; the launch traced here: 156 us
  waiting for transfers between devices  38.9 us (25%)
  starting transfers between devices  38.7 us (25%)
  blocking collectives  28.9 us (18%)
  local copies, waits for them, and re-layouts  18.2 us (12%)
  other arithmetic  17.9 us (11%)
  matrix products  12.8 us (8%)
    all_to_all x3, starting transfers between devices, spread(): lax.all_to_all(jnp.broadcast_to(block[None], (count,) + block.shape), axe...  24.2 us
    all_to_all x3, waiting for transfers between devices, spread(): lax.all_to_all(jnp.broadcast_to(block[None], (count,) + block.shape), axe...  23.9 us
    all_to_all x1, blocking collectives, local(): pieces = lax.all_to_all(pieces, (CORE,) + MODE, 0, 0, tiled=True).sum(0)  13 us
    dot_general x5, matrix products, dot(): lax.dot_general(a, b, (((left,), (right,)), ((), ())), precision=HIGH)  11.8 us
    all_to_all x1, blocking collectives, local(): lax.all_to_all(coeffs.reshape(2, width // 2, count), CORE, 0, 0, tiled=True)  10.3 us
    dot_general x2, local copies, waits for them, and re-layouts, dot(): lax.dot_general(a, b, (((left,), (right,)), ((), ())), precision=HIGH)  10.1 us
    all_to_all x1, waiting for transfers between devices, local(): lax.all_to_all(jnp.broadcast_to(resid[None], (modes, count, part)), MODE,...  8.13 us
    all_to_all x1, waiting for transfers between devices, local(): lax.all_to_all(rotated.reshape(modes, width, part), MODE, 0, 1, tiled=False)  6.86 us
  transfers between devices with their start and end apart: 6, of which 5 were waited for; matrix products, arithmetic and copies ran while one was open for 18% of the time, Pallas kernels for 0%

profile of v1, /device:TPU:1, one launch (start us, length us, event | category | flops | bytes accessed | tf_op | source)
XLA Modules:
  0.0 156.3 jit_solution(13328175090201688889)
XLA Ops:
  0.6 1.8 %fusion.9 = f32[64,64]{1,0:T(8,128)S(1)} fusion(f32[2048,64]{0,1:T(8,128)} %param.3, f32[2048,64]{0,1:T(8,128)} %param.4), kind=kOutput, calls=%fused_computation.20 | convolution fusion | flops 100663296 | bytes 1064960 | tf_op jit(solution)/shard_map/dot_general | solution.py:19
  2.5 10.3 %all_to_all.70 = f32[2,1,2048]{2,1,0:T(1,128)S(1)} all-to-all(f32[2,1,2048]{2,1,0:T(1,128)S(1)} %reshape.39), channel_id=1, replica_groups=mesh['z'=16,'core'=2,'y'=4,'x'=4] {'core'}, dimensions={0} | all-to-all | bytes 32768 | tf_op jit(solution)/shard_map/all_to_all | solution.py:35
  14.9 9.5 %all-to-all-start.3 = ((f32[16,1,2048]{2,1,0:T(1,128)}), f32[16,1,2048]{2,1,0:T(1,128)S(1)}, u32[]{:S(2)}, u32[]{:S(2)}) async-start(f32[16,1,2048]{2,1,0:T(1,128)} %reshape.41), calls=%async_computation.3 | async-start | bytes 262144 | tf_op jit(solution)/shard_map/all_to_all | solution.py:13
  24.5 1.1 copy.29
  25.6 1.0 copy.24
  26.6 10.0 %all-to-all-done.3 = f32[16,1,2048]{2,1,0:T(1,128)S(1)} async-done(((f32[16,1,2048]{2,1,0:T(1,128)}), f32[16,1,2048]{2,1,0:T(1,128)S(1)}, u32[]{:S(2)}, u32[]{:S(2)}) %all-to-all-start.3) | async-done | bytes 131104 | tf_op jit(solution)/shard_map/all_to_all | solution.py:13
  36.6 6.8 %all-to-all-start = ((f32[1,64,16,128]{3,1,0,2:T(8,128)}), f32[1,64,16,128]{3,1,0,2:T(8,128)S(1)}, u32[]{:S(2)}, u32[]{:S(2)}) async-start(f32[1,64,16,128]{3,1,0,2:T(8,128)} %copy.24), calls=%async_computation | async-start | bytes 1048576 | tf_op jit(solution)/shard_map/all_to_all | solution.py:32
  43.4 4.7 %slice_bitcast_fusion = f32[1024,1024]{0,1:T(8,128)} fusion(f32[1088,1024]{1,0:T(8,128)} %param.5), kind=kLoop, calls=%fused_computation | loop fusion | bytes 8388608 | tf_op jit(solution)/shard_map/dot_general | solution.py:19
  48.1 5.3 %copy.23 = f32[1024,1024]{1,0:T(8,128)} copy(f32[1024,1024]{0,1:T(8,128)} %slice_bitcast_fusion) | data formatting | bytes 8388608 | tf_op jit(solution)/shard_map/dot_general | solution.py:19
  53.5 0.9 reduce.7
  54.6 1.0 reshape.43
  55.6 10.8 %all-to-all-start.4 = ((f32[32,1,2048]{2,1,0:T(1,128)}), f32[32,1,2048]{2,1,0:T(1,128)S(1)}, u32[]{:S(2)}, u32[]{:S(2)}) async-start(f32[32,1,2048]{2,1,0:T(1,128)} %reshape.43), calls=%async_computation.4 | async-start | bytes 524288 | tf_op jit(solution)/shard_map/all_to_all | solution.py:13
  66.4 6.4 %convolution_bitcast_fusion = f32[16,64,1,128]{3,1,2,0:T(8,128)} fusion(f32[16,64,1024]{2,1,0:T(8,128)} %bitcast.61, f32[1024,128,1]{1,0,2:T(8,128)S(1)} %bitcast.62), kind=kOutput, calls=%fused_computation.4 | convolution fusion | flops 1610612736 | bytes 5242880 | tf_op jit(solution)/shard_map/dot_general | solution.py:19
  72.8 2.5 %all-to-all-done.4 = f32[32,1,2048]{2,1,0:T(1,128)S(1)} async-done(((f32[32,1,2048]{2,1,0:T(1,128)}), f32[32,1,2048]{2,1,0:T(1,128)S(1)}, u32[]{:S(2)}, u32[]{:S(2)}) %all-to-all-start.4) | async-done | bytes 262176 | tf_op jit(solution)/shard_map/all_to_all | solution.py:13
  75.3 4.2 %all-to-all-start.1 = ((f32[16,64,1,128]{3,1,2,0:T(8,128)}), f32[16,64,1,128]{3,1,2,0:T(8,128)S(1)}, u32[]{:S(2)}, u32[]{:S(2)}) async-start(f32[16,64,1,128]{3,1,2,0:T(8,128)} %convolution_bitcast_fusion), calls=%async_computation.1 | async-start | bytes 1048576 | tf_op jit(solution)/shard_map/all_to_all | solution.py:53
  79.5 1.3 reduce.8
  81.0 1.8 %convolution_subtract_fusion = f32[64,128]{1,0:T(8,128)S(1)} fusion(f32[1024,64]{1,0:T(8,128)S(1)} %bitcast.69, f32[1024,128]{1,0:T(8,128)S(1)} %bitcast.63, f32[2048,64]{0,1:T(8,128)} %param.4, s32[]{:T(128)S(6)} %select_n.10), kind=kOutput, calls=%fused_computation.5 | convolution fusion | flops 100671488 | bytes 851972 | tf_op jit(solution)/shard_map/dot_general | solution.py:19
  83.4 6.9 %all-to-all-done.1 = f32[16,64,1,128]{3,1,2,0:T(8,128)S(1)} async-done(((f32[16,64,1,128]{3,1,2,0:T(8,128)}), f32[16,64,1,128]{3,1,2,0:T(8,128)S(1)}, u32[]{:S(2)}, u32[]{:S(2)}) %all-to-all-start.1) | async-done | bytes 524320 | tf_op jit(solution)/shard_map/all_to_all | solution.py:53
  90.3 13.0 %all_to_all.71 = f32[32,1,2048]{2,1,0:T(1,128)S(1)} all-to-all(f32[32,1,2048]{2,1,0:T(1,128)S(1)} %reshape.45), channel_id=1, replica_groups=mesh['z'=16,'core'=2,'y'=4,'x'=4] {'core','y','x'}, dimensions={0} | all-to-all | bytes 524288 | tf_op jit(solution)/shard_map/all_to_all | solution.py:44
  103.3 0.8 broadcast_in_dim_broadcast_in_dim.2
  104.1 3.6 %all-to-all-start.7 = ((f32[16,64,1,128]{3,1,2,0:T(8,128)}), f32[16,64,1,128]{3,1,2,0:T(8,128)S(1)}, u32[]{:S(2)}, u32[]{:S(2)}) async-start(f32[16,64,1,128]{3,1,2,0:T(8,128)} %broadcast_in_dim_broadcast_in_dim.2), calls=%async_computation.7 | async-start | bytes 1048576 | tf_op jit(solution)/shard_map/all_to_all | solution.py:55
  107.8 1.3 reduce.9
  110.2 8.1 %all-to-all-done.7 = f32[16,64,1,128]{3,1,2,0:T(8,128)S(1)} async-done(((f32[16,64,1,128]{3,1,2,0:T(8,128)}), f32[16,64,1,128]{3,1,2,0:T(8,128)S(1)}, u32[]{:S(2)}, u32[]{:S(2)}) %all-to-all-start.7) | async-done | bytes 524320 | tf_op jit(solution)/shard_map/all_to_all | solution.py:55
  118.3 3.8 %all-to-all-start.6 = ((f32[16,1,2048]{2,1,0:T(1,128)}), f32[16,1,2048]{2,1,0:T(1,128)S(1)}, u32[]{:S(2)}, u32[]{:S(2)}) async-start(f32[16,1,2048]{2,1,0:T(1,128)} %reshape.47), calls=%async_computation.6 | async-start | bytes 262144 | tf_op jit(solution)/shard_map/all_to_all | solution.py:13
  122.8 11.4 %all-to-all-done.6 = f32[16,1,2048]{2,1,0:T(1,128)S(1)} async-done(((f32[16,1,2048]{2,1,0:T(1,128)}), f32[16,1,2048]{2,1,0:T(1,128)S(1)}, u32[]{:S(2)}, u32[]{:S(2)}) %all-to-all-start.6) | async-done | bytes 131104 | tf_op jit(solution)/shard_map/all_to_all | solution.py:13
  134.1 0.9 reduce.10
  135.2 5.6 %all_gather.3 = f32[64,64]{1,0:T(8,128)S(1)} all-gather(f32[32,64]{1,0:T(8,128)S(1)} %reduce_sum.39), channel_id=1, replica_groups=mesh['z'=16,'core'=2,'y'=4,'x'=4] {'core'}, dimensions={0}, use_global_device_ids=true | all-gather | bytes 24576 | tf_op jit(solution)/shard_map/all_gather | solution.py:46
  141.0 5.8 %cholesky.16 = f32[64,64]{1,0:T(8,128)S(1)} custom-call(f32[64,64]{1,0:T(8,128)S(1)} %fusion.7), custom_call_target="Cholesky" | custom-call | tf_op jit(solution)/shard_map/jit(cholesky)/cholesky | solution.py:47
  147.5 1.3 fusion.8
  148.8 4.9 %custom-call.6 = f32[1,64,64]{1,2,0:T(8,128)S(1)} custom-call(f32[1,64,64]{2,1,0:T(8,128)S(1)} %get-tuple-element.3), custom_call_target="InvertDiagBlocksLowerTriangular" | custom-call | tf_op jit(solution)/shard_map/triangular_solve | solution.py:49
  153.7 1.0 fusion.4
  154.7 1.6 %fusion.1 = f32[2048,64]{0,1:T(8,128)} fusion(f32[64,64]{1,0:T(8,128)S(1)} %fusion.4, f32[8,8,16,128]{3,2,1,0:T(8,128)S(1)} %bitcast.65, f32[8,8,16,128]{3,2,1,0:T(8,128)S(1)} %bitcast.64), kind=kOutput, calls=%fused_computation.3 | convolution fusion | flops 100925440 | bytes 1589248 | tf_op jit(solution)/shard_map/dot_general | solution.py:19
  (27 shorter events, 5.8 us)
Async XLA Ops:
  14.9 21.7 %all-to-all-start.3 = ((f32[16,1,2048]{2,1,0:T(1,128)}), f32[16,1,2048]{2,1,0:T(1,128)S(1)}, u32[]{:S(2)}, u32[]{:S(2)}) async-start(f32[16,1,2048]{2,1,0:T(1,128)} %reshape.41), calls=%async_computation.3 | async-start | bytes 262144 | tf_op jit(solution)/shard_map/all_to_all | solution.py:13
  36.6 19.0 %all-to-all-start = ((f32[1,64,16,128]{3,1,0,2:T(8,128)}), f32[1,64,16,128]{3,1,0,2:T(8,128)S(1)}, u32[]{:S(2)}, u32[]{:S(2)}) async-start(f32[1,64,16,128]{3,1,0,2:T(8,128)} %copy.24), calls=%async_computation | async-start | bytes 1048576 | tf_op jit(solution)/shard_map/all_to_all | solution.py:32
  55.6 19.7 %all-to-all-start.4 = ((f32[32,1,2048]{2,1,0:T(1,128)}), f32[32,1,2048]{2,1,0:T(1,128)S(1)}, u32[]{:S(2)}, u32[]{:S(2)}) async-start(f32[32,1,2048]{2,1,0:T(1,128)} %reshape.43), calls=%async_computation.4 | async-start | bytes 524288 | tf_op jit(solution)/shard_map/all_to_all | solution.py:13
  75.3 14.9 %all-to-all-start.1 = ((f32[16,64,1,128]{3,1,2,0:T(8,128)}), f32[16,64,1,128]{3,1,2,0:T(8,128)S(1)}, u32[]{:S(2)}, u32[]{:S(2)}) async-start(f32[16,64,1,128]{3,1,2,0:T(8,128)} %convolution_bitcast_fusion), calls=%async_computation.1 | async-start | bytes 1048576 | tf_op jit(solution)/shard_map/all_to_all | solution.py:53
  104.1 14.2 %all-to-all-start.7 = ((f32[16,64,1,128]{3,1,2,0:T(8,128)}), f32[16,64,1,128]{3,1,2,0:T(8,128)S(1)}, u32[]{:S(2)}, u32[]{:S(2)}) async-start(f32[16,64,1,128]{3,1,2,0:T(8,128)} %broadcast_in_dim_broadcast_in_dim.2), calls=%async_computation.7 | async-start | bytes 1048576 | tf_op jit(solution)/shard_map/all_to_all | solution.py:55
  118.3 15.8 %all-to-all-start.6 = ((f32[16,1,2048]{2,1,0:T(1,128)}), f32[16,1,2048]{2,1,0:T(1,128)S(1)}, u32[]{:S(2)}, u32[]{:S(2)}) async-start(f32[16,1,2048]{2,1,0:T(1,128)} %reshape.47), calls=%async_computation.6 | async-start | bytes 262144 | tf_op jit(solution)/shard_map/all_to_all | solution.py:13

commit v2 on v1

v2 whole, which is shorter than its diff:
```python
import functools

import jax
import jax.numpy as jnp
from jax import lax
from jax.experimental import pallas as pl
from jax.experimental.pallas import tpu as pltpu
from jax.sharding import Mesh, PartitionSpec as P

HIGH = lax.Precision.HIGH
Z = "z"
CORE = "core"
MODE = ("y", "x")


def spread(block, axes, count):
    return lax.all_to_all(
        jnp.broadcast_to(block[None], (count,) + block.shape), axes, 0, 0, tiled=True
    )


def dot(a, b, left, right):
    return lax.dot_general(a, b, (((left,), (right,)), ((), ())), precision=HIGH)


def pack(block):
    half = block.shape[0] // 2
    return jnp.concatenate([block[:half], block[half:]], 1)


def unpack(block):
    half = block.shape[1] // 2
    return jnp.concatenate([block[:, :half], block[:, half:]], 0)


def over_space(block, depth):
    both = lax.all_gather(block, CORE, axis=0, tiled=False).sum(0)
    half = both.shape[0] // 2
    mine = lax.dynamic_slice_in_dim(both, lax.axis_index(CORE) * half, half, 0)
    mine = spread(mine, Z, depth).sum(0)
    return lax.all_gather(mine, CORE, axis=0, tiled=True)


def halves(a):
    top = a.astype(jnp.bfloat16)
    return top, (a - top.astype(jnp.float32)).astype(jnp.bfloat16)


def dot3(a, b, dims=((1,), (0,))):
    (ah, al), (bh, bl) = halves(a), halves(b)
    one = lambda p, q: lax.dot_general(p, q, (dims, ((), ())), preferred_element_type=jnp.float32)
    return one(ah, bh) + (one(ah, bl) + one(al, bh))


def finish(scale, gram_ref, lower_cols_ref, parts_ref, out_ref, factor_ref):
    count = lower_cols_ref.shape[0]
    tiles = count // 8
    packed = gram_ref[...]
    lane = lax.broadcasted_iota(jnp.int32, (8, 2 * count), 1)
    sub = lax.broadcasted_iota(jnp.int32, (8, 2 * count), 0)
    gram = jnp.concatenate([packed[:, :count], packed[:, count:]], 0)
    wide = jnp.concatenate([gram, jnp.zeros((count, count), jnp.float32)], 1)
    rows = [
        jnp.where(lane == sub + (8 * t + count), 1.0, wide[8 * t : 8 * t + 8])
        for t in range(tiles)
    ]
    for j in range(count):
        b, r = divmod(j, 8)
        column = [jnp.broadcast_to(rows[t][:, j : j + 1], (8, 2 * count)) for t in range(b, tiles)]
        pivot = jnp.broadcast_to(column[0][r : r + 1], (8, 2 * count))
        scaled = jnp.broadcast_to(rows[b][r : r + 1], (8, 2 * count)) / pivot
        rows[b] = rows[b] - jnp.where(sub > r, column[0], 0.0) * scaled
        for t in range(b + 1, tiles):
            rows[t] = rows[t] - column[t - b] * scaled
    done = []
    for t in range(tiles):
        diag = jnp.sum(jnp.where(lane == sub + 8 * t, rows[t], 0.0), 1, keepdims=True)
        done.append(jnp.where(lane >= sub + 8 * t, rows[t] * lax.rsqrt(diag), 0.0))
    done = jnp.concatenate(done, 0)
    factor_ref[...] = done[:, :count].T * (1.0 / scale)
    weights = dot3(lower_cols_ref[...].T, done[:, count:]) * scale
    part = parts_ref.shape[2]
    for j in range(parts_ref.shape[0]):
        piece = parts_ref[j]
        out_ref[:, j * part : (j + 1) * part] = piece[:count] * scale + dot3(
            weights, piece[count : 2 * count]
        )


def local(basis, snapshots, rotation):
    depth = lax.axis_size(Z)
    modes = lax.axis_size("y") * lax.axis_size("x")
    rows, width = basis.shape
    count = snapshots.shape[1]
    part = rows // modes
    total = rotation.shape[1]
    place = lax.axis_index(MODE)
    scale = float(rows * depth * 2) ** 0.5
    bt, st = basis.T, snapshots.T
    tiles = bt.reshape(width, modes, part).transpose(1, 0, 2)
    coeffs = over_space(pack(dot(bt, st, 1, 1)), depth)
    coeffs = jnp.broadcast_to(coeffs[None], (modes,) + coeffs.shape)
    got = lax.all_to_all(jnp.concatenate([tiles, coeffs], 1), MODE, 0, 0, tiled=True)
    own = got[:, :width].reshape(total, part)
    coeffs = got[:, width:]
    coeffs = jnp.concatenate([coeffs[:, :, :count], coeffs[:, :, count:]], 1).reshape(total, count)
    resid = lax.dynamic_slice_in_dim(st, place * part, part, 1) - dot(coeffs, own, 0, 0)
    gram = dot(resid, resid, 1, 1)
    rotated = dot(rotation[:total], own, 0, 0).reshape(modes, width, part)
    rest = jnp.concatenate([resid, pack(gram)], 0)
    rest = jnp.broadcast_to(rest[None], (modes,) + rest.shape)
    parts = lax.all_to_all(jnp.concatenate([rotated, rest], 1), MODE, 0, 0, tiled=True)
    gram = over_space(parts[:, width + count :].sum(0), depth)
    lower_cols = lax.dynamic_slice(rotation, (total, place * width), (count, width))
    vmem = pl.BlockSpec(memory_space=pltpu.VMEM)
    out, factor = pl.pallas_call(
        functools.partial(finish, scale),
        out_shape=(
            jax.ShapeDtypeStruct((width, rows), jnp.float32),
            jax.ShapeDtypeStruct((count, count), jnp.float32),
        ),
        in_specs=[vmem] * 3,
        out_specs=(vmem, vmem),
        compiler_params=pltpu.CompilerParams(vmem_limit_bytes=32 << 20),
        name="finish",
    )(gram, lower_cols, parts)
    return out.T, factor


def solution(mesh):
    y, x = 4, 4
    split = Mesh(mesh.devices.reshape(-1, 2, y, x), ("z", "core", "y", "x"))
    space, mode = ("z", "core"), ("y", "x")
    placed = (P(space, mode), P(space, None), P())
    return jax.shard_map(
        local, mesh=split, in_specs=placed, out_specs=(P(space, mode), P()), check_vma=False
    )
```

time: 157 us -> 123 us (0.78)
  starting transfers between devices: 38.7 us -> 20.2 us
  other arithmetic: 17.9 us -> 1.25 us
  blocking collectives: 28.9 us -> 43.7 us
  local copies, waits for them, and re-layouts: 18.2 us -> 3.73 us
  Pallas kernels: 0 us -> 9.71 us
  matrix products: 12.8 us -> 6.47 us
  waiting for transfers between devices: 38.9 us -> 37 us
    all_gather x1 -> x4, blocking collectives: 5.64 us -> 21.4 us  [the longest x2 11.9 us: over_space(): both = lax.all_gather(block, CORE, axis=0, tiled=False).sum(0)]
    another operation x4 -> x0, other arithmetic: 11.4 us -> none  [the longest x3 6.52 us: local(): lower = jnp.linalg.cholesky(gram)]
    all_to_all x3 -> x2, starting transfers between devices: 24.2 us -> 13.4 us  [spread(): lax.all_to_all(jnp.broadcast_to(block[None], (count,) + block.shape), axe...]
    dot_general x2 -> x1, local copies, waits for them, and re-layouts: 10.1 us -> 0.19 us  [dot(): lax.dot_general(a, b, (((left,), (right,)), ((), ())), precision=HIGH)]
    pallas_call x0 -> x1, Pallas kernels: none -> 9.71 us  [local(): pl.pallas_call(functools.partial(finish, scale), out_shape=(jax.ShapeDtyp...]
    all_to_all x3 -> x1, starting transfers between devices: 14.6 us -> 6.75 us  [local(): lax.all_to_all(jnp.concatenate([tiles, coeffs], 1), MODE, 0, 0, tiled=True)]
    dot_general x5 -> x4, matrix products: 11.8 us -> 6.47 us  [dot(): lax.dot_general(a, b, (((left,), (right,)), ((), ())), precision=HIGH)]
    all_to_all x5 -> x0, other arithmetic: 5.11 us -> none  [the longest x3 3.16 us: spread(): lax.all_to_all(jnp.broadcast_to(block[None], (count,) + block.shape), axe...]
  transfers between devices with their start and end apart: 6 -> 3, of which waited for: 5 -> 3; matrix products, arithmetic and copies ran while one was open for 18% -> 1% of each run, Pallas kernels for 0% -> 0%
where the time goes in v2:
time: 123 us
  blocking collectives  43.7 us (36%)
  waiting for transfers between devices  37 us (30%)
  starting transfers between devices  20.2 us (16%)
  Pallas kernels  9.71 us (8%)
  matrix products  6.47 us (5%)
  local copies, waits for them, and re-layouts  3.73 us (3%)
  other arithmetic  1.25 us (1%)
    all_to_all x2, waiting for transfers between devices, spread(): lax.all_to_all(jnp.broadcast_to(block[None], (count,) + block.shape), axe...  23.4 us
    all_to_all x1, blocking collectives, local(): lax.all_to_all(jnp.concatenate([rotated, rest], 1), MODE, 0, 0, tiled=True)  22.3 us
    all_to_all x1, waiting for transfers between devices, local(): lax.all_to_all(jnp.concatenate([tiles, coeffs], 1), MODE, 0, 0, tiled=True)  13.6 us
    all_to_all x2, starting transfers between devices, spread(): lax.all_to_all(jnp.broadcast_to(block[None], (count,) + block.shape), axe...  13.4 us
    all_gather x2, blocking collectives, over_space(): both = lax.all_gather(block, CORE, axis=0, tiled=False).sum(0)  11.9 us
    pallas_call x1, Pallas kernels, local(): pl.pallas_call(functools.partial(finish, scale), out_shape=(jax.ShapeDtyp...  9.71 us
    all_gather x2, blocking collectives, over_space(): return lax.all_gather(mine, CORE, axis=0, tiled=True)  9.47 us
    all_to_all x1, starting transfers between devices, local(): lax.all_to_all(jnp.concatenate([tiles, coeffs], 1), MODE, 0, 0, tiled=True)  6.75 us
  transfers between devices with their start and end apart: 3, of which 3 were waited for; matrix products, arithmetic and copies ran while one was open for 1% of the time, Pallas kernels for 0%

profile of v2, /device:TPU:1, one launch (start us, length us, event | category | flops | bytes accessed | tf_op | source)
XLA Modules:
  0.0 122.8 jit_solution(17675158940929791163)
XLA Ops:
  0.6 0.0 copy-start
  0.6 1.0 copy-done
  1.7 1.4 %fusion.14 = f32[64,64]{1,0:T(8,128)S(1)} fusion(f32[2048,64]{0,1:T(8,128)S(1)} %copy-done, f32[2048,64]{0,1:T(8,128)} %param.4), kind=kOutput, calls=%fused_computation.22 | convolution fusion | flops 50331648 | bytes 1064960 | tf_op jit(solution)/shard_map/dot_general | solution.py:23
  3.1 0.1 pad_maximum_fusion.2
  3.2 8.4 %all-gather = f32[64,128]{1,0:T(8,128)S(1)} all-gather(f32[32,128]{1,0:T(8,128)S(1)} %pad_maximum_fusion.2), channel_id=2, replica_groups=mesh['z'=16,'core'=2,'y'=4,'x'=4] {'core'}, dimensions={0}, use_global_device_ids=true | all-gather | bytes 49152 | tf_op jit(solution)/shard_map/all_gather | solution.py:37
  11.5 0.7 broadcast_in_dim.8
  12.2 9.5 %all-to-all-start = ((f32[16,16,128]{2,1,0:T(8,128)}), f32[16,16,128]{2,1,0:T(8,128)S(1)}, u32[]{:S(2)}, u32[]{:S(2)}) async-start(f32[16,16,128]{2,1,0:T(8,128)} %broadcast_in_dim.8), calls=%async_computation | async-start | bytes 262144 | tf_op jit(solution)/shard_map/all_to_all | solution.py:17
  21.8 12.1 %all-to-all-done = f32[16,16,128]{2,1,0:T(8,128)S(1)} async-done(((f32[16,16,128]{2,1,0:T(8,128)}), f32[16,16,128]{2,1,0:T(8,128)S(1)}, u32[]{:S(2)}, u32[]{:S(2)}) %all-to-all-start) | async-done | bytes 131104 | tf_op jit(solution)/shard_map/all_to_all | solution.py:17
  33.9 4.7 %all_gather.20 = f32[32,128]{1,0:T(8,128)S(1)} all-gather(f32[16,128]{1,0:T(8,128)S(1)} %reduce_sum.46), channel_id=1, replica_groups=mesh['z'=16,'core'=2,'y'=4,'x'=4] {'core'}, dimensions={0}, use_global_device_ids=true | all-gather | bytes 24576 | tf_op jit(solution)/shard_map/all_gather | solution.py:41
  38.7 0.9 pad_maximum_fusion.1
  39.6 6.8 %all-to-all-start.1 = ((f32[16,96,128]{2,1,0:T(8,128)}), f32[16,96,128]{2,1,0:T(8,128)S(1)}, u32[]{:S(2)}, u32[]{:S(2)}) async-start(f32[16,96,128]{2,1,0:T(8,128)} %pad_maximum_fusion.1), calls=%async_computation.1 | async-start | bytes 1572864 | tf_op jit(solution)/shard_map/all_to_all | solution.py:103
  46.4 13.6 %all-to-all-done.1 = f32[16,96,128]{2,1,0:T(8,128)S(1)} async-done(((f32[16,96,128]{2,1,0:T(8,128)}), f32[16,96,128]{2,1,0:T(8,128)S(1)}, u32[]{:S(2)}, u32[]{:S(2)}) %all-to-all-start.1) | async-done | bytes 786464 | tf_op jit(solution)/shard_map/all_to_all | solution.py:103
  60.0 0.1 fusion.11
  60.1 1.4 %fusion.5 = f32[64,128]{1,0:T(8,128)S(1)} fusion(f32[16,32,64]{2,1,0:T(8,128)S(1)} %get-tuple-element.7, f32[16,32,64]{2,1,0:T(8,128)S(1)} %get-tuple-element.6, f32[2048,64]{0,1:T(8,128)} %param.4, s32[]{:T(128)S(6)} %select_n.11, f32[16,96,128]{2,1,0:T(8,128)S(1)} %all-to-all-done.1), kind=kOutput, calls=%fused_computation.5 | convolution fusion | flops 50405376 | bytes 1114116 | tf_op jit(solution)/shard_map/dot_general | solution.py:23
  61.5 0.2 fusion.15
  61.7 3.6 %fusion.2 = f32[1024,128]{0,1:T(8,128)S(1)} fusion(f32[1024,128]{1,0:T(8,128)S(1)} %bitcast.27, f32[1088,1024]{1,0:T(8,128)} %param.5), kind=kOutput, calls=%fused_computation.3 | convolution fusion | flops 805306368 | bytes 5242880 | tf_op jit(solution)/shard_map/dot_general | solution.py:23
  65.3 0.2 copy.11
  65.5 0.1 maximum_maximum_fusion
  65.5 0.1 broadcast_in_dim.10
  65.6 0.1 pad_maximum_fusion
  65.7 22.3 %all_to_all.20.parts_ref = f32[16,160,128]{2,1,0:T(8,128)S(1)} all-to-all(f32[16,160,128]{2,1,0:T(8,128)S(1)} %pad_maximum_fusion), channel_id=1, replica_groups=mesh['z'=16,'core'=2,'y'=4,'x'=4] {'y','x'}, dimensions={0} | all-to-all | bytes 2621440 | tf_op jit(solution)/shard_map/all_to_all | solution.py:112
  88.0 3.6 %all-gather.1 = f32[64,128]{1,0:T(8,128)S(1)} all-gather(f32[32,128]{1,0:T(8,128)S(1)} %slice_reduce_fusion), channel_id=3, replica_groups=mesh['z'=16,'core'=2,'y'=4,'x'=4] {'core'}, dimensions={0}, use_global_device_ids=true | all-gather | bytes 49152 | tf_op jit(solution)/shard_map/all_gather | solution.py:37
  91.6 0.7 broadcast_in_dim.11
  92.3 3.9 %all-to-all-start.3 = ((f32[16,16,128]{2,1,0:T(8,128)}), f32[16,16,128]{2,1,0:T(8,128)S(1)}, u32[]{:S(2)}, u32[]{:S(2)}) async-start(f32[16,16,128]{2,1,0:T(8,128)} %broadcast_in_dim.11), calls=%async_computation.3 | async-start | bytes 262144 | tf_op jit(solution)/shard_map/all_to_all | solution.py:17
  96.2 0.8 constant_dynamic-slice_fusion.2.lower_cols_ref
  97.0 11.3 %all-to-all-done.3 = f32[16,16,128]{2,1,0:T(8,128)S(1)} async-done(((f32[16,16,128]{2,1,0:T(8,128)}), f32[16,16,128]{2,1,0:T(8,128)S(1)}, u32[]{:S(2)}, u32[]{:S(2)}) %all-to-all-start.3) | async-done | bytes 131104 | tf_op jit(solution)/shard_map/all_to_all | solution.py:17
  108.3 4.7 %all_gather.23.gram_ref = f32[32,128]{1,0:T(8,128)S(1)} all-gather(f32[16,128]{1,0:T(8,128)S(1)} %reduce_sum.49), channel_id=1, replica_groups=mesh['z'=16,'core'=2,'y'=4,'x'=4] {'core'}, dimensions={0}, use_global_device_ids=true | all-gather | bytes 24576 | tf_op jit(solution)/shard_map/all_gather | solution.py:41
  113.1 9.7 %finish.1 = (f32[64,2048]{1,0:T(8,128)}, f32[64,64]{1,0:T(8,128)}) custom-call(f32[32,128]{1,0:T(8,128)S(1)} %all_gather.23.gram_ref, f32[64,64]{1,0:T(8,128)S(1)} %constant_dynamic-slice_fusion.2.lower_cols_ref, f32[16,160,128]{2,1,0:T(8,128)S(1)} %all_to_all.20.parts_ref), custom_call_target="tpu_custom_call" | custom-call | tf_op jit(solution)/shard_map/finish/pallas_call | solution.py:116
  (12 shorter events, 0.2 us)
Async XLA Ops:
  0.6 1.0 copy-start
  12.2 21.7 %all-to-all-start = ((f32[16,16,128]{2,1,0:T(8,128)}), f32[16,16,128]{2,1,0:T(8,128)S(1)}, u32[]{:S(2)}, u32[]{:S(2)}) async-start(f32[16,16,128]{2,1,0:T(8,128)} %broadcast_in_dim.8), calls=%async_computation | async-start | bytes 262144 | tf_op jit(solution)/shard_map/all_to_all | solution.py:17
  39.6 20.3 %all-to-all-start.1 = ((f32[16,96,128]{2,1,0:T(8,128)}), f32[16,96,128]{2,1,0:T(8,128)S(1)}, u32[]{:S(2)}, u32[]{:S(2)}) async-start(f32[16,96,128]{2,1,0:T(8,128)} %pad_maximum_fusion.1), calls=%async_computation.1 | async-start | bytes 1572864 | tf_op jit(solution)/shard_map/all_to_all | solution.py:103
  92.3 16.0 %all-to-all-start.3 = ((f32[16,16,128]{2,1,0:T(8,128)}), f32[16,16,128]{2,1,0:T(8,128)S(1)}, u32[]{:S(2)}, u32[]{:S(2)}) async-start(f32[16,16,128]{2,1,0:T(8,128)} %broadcast_in_dim.11), calls=%async_computation.3 | async-start | bytes 262144 | tf_op jit(solution)/shard_map/all_to_all | solution.py:17

commit v3 on v1

v3 whole, which is shorter than its diff:
```python
import functools

import jax
import jax.numpy as jnp
from jax import lax
from jax.experimental import pallas as pl
from jax.experimental.pallas import tpu as pltpu
from jax.sharding import Mesh, PartitionSpec as P

HIGH = lax.Precision.HIGH
Z = "z"
CORE = "core"
MODE = ("y", "x")
STEP = 8
CHUNKS = 4
VMEM = pl.BlockSpec(memory_space=pltpu.VMEM)
ANY = pl.BlockSpec(memory_space=pl.ANY)
LIMIT = pltpu.CompilerParams(vmem_limit_bytes=32 << 20)


def struct(*shape):
    return jax.ShapeDtypeStruct(shape, jnp.float32)


def spread(block, axes, count):
    return lax.all_to_all(
        jnp.broadcast_to(block[None], (count,) + block.shape), axes, 0, 0, tiled=True
    )


def dot(a, b, left, right):
    return lax.dot_general(a, b, (((left,), (right,)), ((), ())), precision=HIGH)


def halves(a):
    top = a.astype(jnp.bfloat16)
    return top, (a - top.astype(jnp.float32)).astype(jnp.bfloat16)


def dot3(a, b, left=1, right=0):
    (ah, al), (bh, bl) = halves(a), halves(b)

    def one(p, q):
        dims = (((left,), (right,)), ((), ()))
        return lax.dot_general(p, q, dims, preferred_element_type=jnp.float32)

    return one(ah, bh) + (one(ah, bl) + one(al, bh))


def pack(block):
    half = block.shape[0] // 2
    return jnp.concatenate([block[:half], block[half:]], 1)


def project(bt_ref, st_ref, out_ref, b_buf, s_buf, sems):
    step = b_buf.shape[1] // CHUNKS
    copies = []
    for i in range(CHUNKS):
        cut = pl.ds(i * step, step)
        for k, (src, dst) in enumerate(((bt_ref, b_buf), (st_ref, s_buf))):
            copy = pltpu.make_async_copy(src.at[:, cut], dst.at[:, cut], sems.at[2 * i + k])
            copy.start()
            copies.append(copy)
    total = None
    for i in range(CHUNKS):
        copies[2 * i].wait()
        copies[2 * i + 1].wait()
        cut = slice(i * step, (i + 1) * step)
        term = dot3(b_buf[:, cut], s_buf[:, cut], 1, 1)
        total = term if total is None else total + term
    out_ref[...] = pack(total)


def remainder(got_ref, st_ref, resid_ref, gram_ref):
    modes, _, part = got_ref.shape
    count = st_ref.shape[0]
    width = got_ref.shape[1] - count // 2
    half = width // 2
    got = got_ref[...]
    upper = got[:, :half].reshape(modes * half, part)
    lower = got[:, half:width].reshape(modes * half, part)
    coeffs = got[:, width:].reshape(modes * half, 2 * count)
    both = dot3(coeffs.T, jnp.concatenate([upper, lower], 1))
    resid = st_ref[...] - (both[:count, :part] + both[count:, part:])
    resid_ref[...] = resid
    gram_ref[...] = pack(dot3(resid, resid, 1, 1))


def eliminate(gram):
    count = gram.shape[0]
    tiles = count // STEP
    shape = (STEP, 2 * count)
    lane = lax.broadcasted_iota(jnp.int32, shape, 1)
    sub = lax.broadcasted_iota(jnp.int32, shape, 0)
    wide = jnp.concatenate([gram, jnp.zeros((count, count), jnp.float32)], 1)
    rows = [
        jnp.where(lane == sub + (STEP * t + count), 1.0, wide[STEP * t : STEP * (t + 1)])
        for t in range(tiles)
    ]
    done = []
    for b in range(tiles):
        later = range(b + 1, tiles)
        first = STEP * b
        block = [
            jnp.broadcast_to(rows[b][:, first + k : first + k + 1], shape) for k in range(STEP)
        ]
        column = [
            {t: jnp.broadcast_to(rows[t][:, first + k : first + k + 1], shape) for t in later}
            for k in range(STEP)
        ]
        row = [jnp.broadcast_to(rows[b][k : k + 1], shape) for k in range(STEP)]
        pivot = {
            (i, k): jnp.broadcast_to(block[k][i : i + 1], shape)
            for i in range(STEP)
            for k in range(i + 1)
        }
        scaled = []
        for k in range(STEP):
            inverse = 1.0 / pivot[k, k]
            scaled.append(row[k] * inverse)
            for i in range(k + 1, STEP):
                ratio = pivot[i, k] * inverse
                for m in range(k + 1, i + 1):
                    pivot[i, m] = pivot[i, m] - ratio * pivot[m, k]
                row[i] = row[i] - ratio * row[k]
                for t in later:
                    column[i][t] = column[i][t] - ratio * column[k][t]
        for t in later:
            for k in range(STEP):
                rows[t] = rows[t] - column[k][t] * scaled[k]
        final = jnp.zeros(shape, jnp.float32)
        for k in range(STEP):
            final = jnp.where(sub == k, row[k] * lax.rsqrt(pivot[k, k]), final)
        done.append(jnp.where(lane >= sub + first, final, 0.0))
    return jnp.concatenate(done, 0)


def finish(scale, gram_ref, lower_cols_ref, parts_ref, out_ref, factor_ref):
    count = lower_cols_ref.shape[0]
    packed = gram_ref[...]
    done = eliminate(jnp.concatenate([packed[:, :count], packed[:, count:]], 0))
    factor_ref[...] = done[:, :count].T * (1.0 / scale)
    weights = dot3(lower_cols_ref[...].T, done[:, count:]) * scale
    modes, _, part = parts_ref.shape
    for j in range(modes):
        piece = parts_ref[j]
        out_ref[:, j * part : (j + 1) * part] = piece[:count] * scale + dot3(
            weights, piece[count : 2 * count]
        )


def core_half(block):
    both = lax.all_gather(block, CORE, axis=0, tiled=False).sum(0)
    half = both.shape[0] // 2
    return lax.dynamic_slice_in_dim(both, lax.axis_index(CORE) * half, half, 0)


def local(basis, snapshots, rotation):
    depth = lax.axis_size(Z)
    modes = lax.axis_size("y") * lax.axis_size("x")
    rows, width = basis.shape
    count = snapshots.shape[1]
    part = rows // modes
    total = rotation.shape[1]
    place = lax.axis_index(MODE)
    scale = float(rows * depth * 2) ** 0.5
    bt, st = basis.T, snapshots.T
    coeffs = pl.pallas_call(
        project,
        out_shape=struct(width // 2, 2 * count),
        in_specs=[ANY, ANY],
        out_specs=VMEM,
        scratch_shapes=[
            pltpu.VMEM((width, rows), jnp.float32),
            pltpu.VMEM((count, rows), jnp.float32),
            pltpu.SemaphoreType.DMA((2 * CHUNKS,)),
        ],
        compiler_params=LIMIT,
        name="project",
    )(bt, st)
    coeffs = spread(core_half(coeffs), Z, depth).sum(0)
    coeffs = lax.all_gather(coeffs, CORE, axis=0, tiled=True)
    pieces = bt.reshape(width, modes, part).transpose(1, 0, 2)
    pieces = jnp.concatenate([pieces, jnp.zeros((modes, width // 2, part), jnp.float32)], 1)
    pieces = lax.dynamic_update_slice(
        pieces, jnp.broadcast_to(coeffs[None], (modes,) + coeffs.shape), (0, width, 0)
    )
    got = lax.all_to_all(pieces, MODE, 0, 0, tiled=True)
    resid, gram = pl.pallas_call(
        remainder,
        out_shape=(struct(count, part), struct(count // 2, 2 * count)),
        in_specs=[VMEM, VMEM],
        out_specs=(VMEM, VMEM),
        compiler_params=LIMIT,
        name="remainder",
    )(got, lax.dynamic_slice_in_dim(st, place * part, part, 1))
    gram = spread(core_half(gram), Z, depth).sum(0)
    own = got[:, :width].reshape(total, part)
    rotated = dot(rotation[:total], own, 0, 0).reshape(modes, width, part)
    resid = jnp.broadcast_to(resid[None], (modes,) + resid.shape)
    empty = jnp.zeros((modes,) + gram.shape, jnp.float32)
    pieces = lax.dynamic_update_slice(
        jnp.concatenate([rotated, resid, empty], 1),
        jnp.broadcast_to(gram[None], (modes,) + gram.shape),
        (0, width + count, 0),
    )
    parts = lax.all_to_all(pieces, MODE, 0, 0, tiled=True)
    gram = lax.all_gather(parts[:, width + count :].sum(0), CORE, axis=0, tiled=True)
    lower_cols = lax.dynamic_slice(rotation, (total, place * width), (count, width))
    out, factor = pl.pallas_call(
        functools.partial(finish, scale),
        out_shape=(struct(width, rows), struct(count, count)),
        in_specs=[VMEM] * 3,
        out_specs=(VMEM, VMEM),
        compiler_params=LIMIT,
        name="finish",
    )(gram, lower_cols, parts)
    return out.T, factor


def solution(mesh):
    y, x = 4, 4
    split = Mesh(mesh.devices.reshape(-1, 2, y, x), ("z", "core", "y", "x"))
    space, mode = ("z", "core"), ("y", "x")
    placed = (P(space, mode), P(space, None), P())
    return jax.shard_map(
        local, mesh=split, in_specs=placed, out_specs=(P(space, mode), P()), check_vma=False
    )
```

time: 157 us -> 111 us (0.71)
  other arithmetic: 17.9 us -> 2.16 us
  starting transfers between devices: 38.7 us -> 23.8 us
  local copies, waits for them, and re-layouts: 18.2 us -> 6.06 us
  matrix products: 12.8 us -> 3.55 us
  waiting for transfers between devices: 38.9 us -> 46.7 us
  blocking collectives: 28.9 us -> 22.4 us
  Pallas kernels: 0 us -> 4.76 us
    all_to_all x2 -> x0, blocking collectives: 23.3 us -> none  [the longest x1 13 us: local(): pieces = lax.all_to_all(pieces, (CORE,) + MODE, 0, 0, tiled=True).sum(0)]
    all_gather x1 -> x4, blocking collectives: 5.64 us -> 22.4 us  [the longest x2 11.6 us: core_half(): both = lax.all_gather(block, CORE, axis=0, tiled=False).sum(0)]
    all_to_all x3 -> x2, waiting for transfers between devices: 15 us -> 27.5 us  [the longest x1 14.7 us: local(): parts = lax.all_to_all(pieces, MODE, 0, 0, tiled=True)]
    another operation x4 -> x0, other arithmetic: 11.4 us -> none  [the longest x3 6.52 us: local(): lower = jnp.linalg.cholesky(gram)]
    all_to_all x3 -> x2, starting transfers between devices: 24.2 us -> 13.4 us  [spread(): lax.all_to_all(jnp.broadcast_to(block[None], (count,) + block.shape), axe...]
    dot_general x2 -> x1, local copies, waits for them, and re-layouts: 10.1 us -> 0.19 us  [dot(): lax.dot_general(a, b, (((left,), (right,)), ((), ())), precision=HIGH)]
    dot_general x5 -> x1, matrix products: 11.8 us -> 3.55 us  [dot(): lax.dot_general(a, b, (((left,), (right,)), ((), ())), precision=HIGH)]
    all_to_all x5 -> x0, other arithmetic: 5.11 us -> none  [the longest x3 3.16 us: spread(): lax.all_to_all(jnp.broadcast_to(block[None], (count,) + block.shape), axe...]
  transfers between devices with their start and end apart: 6 -> 4, of which waited for: 5 -> 4; matrix products, arithmetic and copies ran while one was open for 18% -> 6% of each run, Pallas kernels for 0% -> 0%
where the time goes in v3:
time: 111 us; the launch traced here: 110 us
  waiting for transfers between devices  46.7 us (42%)
  starting transfers between devices  23.8 us (21%)
  blocking collectives  22.4 us (20%)
  local copies, waits for them, and re-layouts  6.06 us (5%)
  Pallas kernels  4.76 us (4%)
  matrix products  3.55 us (3%)
  other arithmetic  2.16 us (2%)
    all_to_all x2, waiting for transfers between devices, spread(): lax.all_to_all(jnp.broadcast_to(block[None], (count,) + block.shape), axe...  19.2 us
    all_to_all x1, waiting for transfers between devices, local(): parts = lax.all_to_all(pieces, MODE, 0, 0, tiled=True)  14.7 us
    all_to_all x2, starting transfers between devices, spread(): lax.all_to_all(jnp.broadcast_to(block[None], (count,) + block.shape), axe...  13.4 us
    all_to_all x1, waiting for transfers between devices, local(): got = lax.all_to_all(pieces, MODE, 0, 0, tiled=True)  12.8 us
    all_gather x2, blocking collectives, core_half(): both = lax.all_gather(block, CORE, axis=0, tiled=False).sum(0)  11.6 us
    all_to_all x1, starting transfers between devices, local(): got = lax.all_to_all(pieces, MODE, 0, 0, tiled=True)  6.75 us
    all_gather x1, blocking collectives, local(): lax.all_gather(parts[:, width + count:].sum(0), CORE, axis=0, tiled=True)  6.04 us
    all_gather x1, blocking collectives, local(): coeffs = lax.all_gather(coeffs, CORE, axis=0, tiled=True)  4.74 us
  transfers between devices with their start and end apart: 4, of which 4 were waited for; matrix products, arithmetic and copies ran while one was open for 6% of the time, Pallas kernels for 0%

profile of v3, /device:TPU:1, one launch (start us, length us, event | category | flops | bytes accessed | tf_op | source)
XLA Modules:
  0.0 110.2 jit_solution(6083212370787419010)
XLA Ops:
  0.6 0.0 copy-start
  0.6 1.0 copy-done
  1.7 0.0 copy-start.2
  1.7 1.0 copy-done.2
  2.7 0.0 copy-start.1
  2.7 1.0 project.1
  3.8 8.4 %all-gather = f32[64,128]{1,0:T(8,128)S(1)} all-gather(f32[32,128]{1,0:T(8,128)S(1)} %project.1), channel_id=2, replica_groups=mesh['z'=16,'core'=2,'y'=4,'x'=4] {'core'}, dimensions={0}, use_global_device_ids=true | all-gather | bytes 49152 | tf_op jit(solution)/shard_map/all_gather | solution.py:153
  12.1 0.7 broadcast_in_dim.12
  12.8 9.5 %all-to-all-start = ((f32[16,16,128]{2,1,0:T(8,128)}), f32[16,16,128]{2,1,0:T(8,128)S(1)}, u32[]{:S(2)}, u32[]{:S(2)}) async-start(f32[16,16,128]{2,1,0:T(8,128)} %broadcast_in_dim.12), calls=%async_computation | async-start | bytes 262144 | tf_op jit(solution)/shard_map/all_to_all | solution.py:26
  22.4 0.0 copy-done.1
  22.4 12.1 %all-to-all-done = f32[16,16,128]{2,1,0:T(8,128)S(1)} async-done(((f32[16,16,128]{2,1,0:T(8,128)}), f32[16,16,128]{2,1,0:T(8,128)S(1)}, u32[]{:S(2)}, u32[]{:S(2)}) %all-to-all-start) | async-done | bytes 131104 | tf_op jit(solution)/shard_map/all_to_all | solution.py:26
  34.5 4.7 %all_gather.20 = f32[32,128]{1,0:T(8,128)S(1)} all-gather(f32[16,128]{1,0:T(8,128)S(1)} %reduce_sum.46), channel_id=1, replica_groups=mesh['z'=16,'core'=2,'y'=4,'x'=4] {'core'}, dimensions={0}, use_global_device_ids=true | all-gather | bytes 24576 | tf_op jit(solution)/shard_map/all_gather | solution.py:182
  39.3 0.9 pad_maximum_fusion
  40.2 6.8 %all-to-all-start.1 = ((f32[16,96,128]{2,1,0:T(8,128)}), f32[16,96,128]{2,1,0:T(8,128)S(1)}, u32[]{:S(2)}, u32[]{:S(2)}) async-start(f32[16,96,128]{2,1,0:T(8,128)} %pad_maximum_fusion), calls=%async_computation.1 | async-start | bytes 1572864 | tf_op jit(solution)/shard_map/all_to_all | solution.py:188
  47.0 0.8 dynamic-slice_bitcast_fusion.st_ref
  47.8 12.8 %all-to-all-done.1.got_ref = f32[16,96,128]{2,1,0:T(8,128)S(1)} async-done(((f32[16,96,128]{2,1,0:T(8,128)}), f32[16,96,128]{2,1,0:T(8,128)S(1)}, u32[]{:S(2)}, u32[]{:S(2)}) %all-to-all-start.1) | async-done | bytes 786464 | tf_op jit(solution)/shard_map/all_to_all | solution.py:188
  60.6 0.5 remainder.1
  61.1 3.3 %all-gather.1 = f32[64,128]{1,0:T(8,128)S(1)} all-gather(f32[32,128]{1,0:T(8,128)S(1)} %get-tuple-element.7), channel_id=3, replica_groups=mesh['z'=16,'core'=2,'y'=4,'x'=4] {'core'}, dimensions={0}, use_global_device_ids=true | all-gather | bytes 49152 | tf_op jit(solution)/shard_map/all_gather | solution.py:153
  64.4 0.7 broadcast_in_dim.16
  65.0 3.8 %all-to-all-start.2 = ((f32[16,16,128]{2,1,0:T(8,128)}), f32[16,16,128]{2,1,0:T(8,128)S(1)}, u32[]{:S(2)}, u32[]{:S(2)}) async-start(f32[16,16,128]{2,1,0:T(8,128)} %broadcast_in_dim.16), calls=%async_computation.2 | async-start | bytes 262144 | tf_op jit(solution)/shard_map/all_to_all | solution.py:26
  68.9 3.6 %fusion.2 = f32[1024,128]{0,1:T(8,128)S(1)} fusion(f32[1024,128]{1,0:T(8,128)S(1)} %bitcast.21, f32[1088,1024]{1,0:T(8,128)} %param.5), kind=kOutput, calls=%fused_computation.2 | convolution fusion | flops 805306368 | bytes 5242880 | tf_op jit(solution)/shard_map/dot_general | solution.py:32
  72.5 0.2 copy.9
  72.7 1.2 %maximum_maximum_fusion = f32[16,144,128]{2,1,0:T(8,128)} fusion(f32[16,64,128]{2,1,0:T(8,128)S(1)} %broadcast_in_dim.14, f32[16,64,128]{2,1,0:T(8,128)S(1)} %bitcast.22, f32[144]{0:T(256)S(1)} %pad.3.clone), kind=kLoop, calls=%fused_computation.3 | loop fusion | flops 589824 | bytes 2228800 | tf_op jit(solution)/shard_map/concatenate | solution.py:203
  73.9 7.1 %all-to-all-done.2 = f32[16,16,128]{2,1,0:T(8,128)S(1)} async-done(((f32[16,16,128]{2,1,0:T(8,128)}), f32[16,16,128]{2,1,0:T(8,128)S(1)}, u32[]{:S(2)}, u32[]{:S(2)}) %all-to-all-start.2) | async-done | bytes 131104 | tf_op jit(solution)/shard_map/all_to_all | solution.py:26
  81.0 0.7 broadcast_dynamic-update-slice_fusion
  81.7 3.7 %all-to-all-start.3 = ((f32[16,144,128]{2,1,0:T(8,128)}), f32[16,144,128]{2,1,0:T(8,128)S(1)}, u32[]{:S(2)}, u32[]{:S(2)}) async-start(f32[16,144,128]{2,1,0:T(8,128)} %broadcast_dynamic-update-slice_fusion), calls=%async_computation.3 | async-start | bytes 2359296 | tf_op jit(solution)/shard_map/all_to_all | solution.py:207
  85.4 0.8 constant_dynamic-slice_fusion.2.lower_cols_ref
  86.2 14.7 %all-to-all-done.3.parts_ref = f32[16,144,128]{2,1,0:T(8,128)S(1)} async-done(((f32[16,144,128]{2,1,0:T(8,128)}), f32[16,144,128]{2,1,0:T(8,128)S(1)}, u32[]{:S(2)}, u32[]{:S(2)}) %all-to-all-start.3) | async-done | bytes 1179680 | tf_op jit(solution)/shard_map/all_to_all | solution.py:207
  101.0 6.0 %all_gather.23.gram_ref = f32[32,128]{1,0:T(8,128)S(1)} all-gather(f32[16,128]{1,0:T(8,128)S(1)} %slice_reduce_fusion), channel_id=1, replica_groups=mesh['z'=16,'core'=2,'y'=4,'x'=4] {'core'}, dimensions={0}, use_global_device_ids=true | all-gather | bytes 24576 | tf_op jit(solution)/shard_map/all_gather | solution.py:208
  107.0 3.2 %finish.1 = (f32[64,2048]{1,0:T(8,128)}, f32[64,64]{1,0:T(8,128)}) custom-call(f32[32,128]{1,0:T(8,128)S(1)} %all_gather.23.gram_ref, f32[64,64]{1,0:T(8,128)S(1)} %constant_dynamic-slice_fusion.2.lower_cols_ref, f32[16,144,128]{2,1,0:T(8,128)S(1)} %all-to-all-done.3.parts_ref), custom_call_target="tpu_custom_call" | custom-call | tf_op jit(solution)/shard_map/finish/pallas_call | solution.py:210
  (13 shorter events, 0.2 us)
Async XLA Ops:
  0.6 1.0 copy-start
  1.7 1.0 copy-start.2
  2.7 19.6 %copy-start.1 = (f32[2048,64]{0,1:T(8,128)S(1)}, f32[2048,64]{0,1:T(8,128)}, u32[]{:S(2)}) copy-start(f32[2048,64]{0,1:T(8,128)} %param.3) | copy-start | bytes 1572868
  12.8 21.7 %all-to-all-start = ((f32[16,16,128]{2,1,0:T(8,128)}), f32[16,16,128]{2,1,0:T(8,128)S(1)}, u32[]{:S(2)}, u32[]{:S(2)}) async-start(f32[16,16,128]{2,1,0:T(8,128)} %broadcast_in_dim.12), calls=%async_computation | async-start | bytes 262144 | tf_op jit(solution)/shard_map/all_to_all | solution.py:26
  40.2 20.3 %all-to-all-start.1 = ((f32[16,96,128]{2,1,0:T(8,128)}), f32[16,96,128]{2,1,0:T(8,128)S(1)}, u32[]{:S(2)}, u32[]{:S(2)}) async-start(f32[16,96,128]{2,1,0:T(8,128)} %pad_maximum_fusion), calls=%async_computation.1 | async-start | bytes 1572864 | tf_op jit(solution)/shard_map/all_to_all | solution.py:188
  65.0 16.0 %all-to-all-start.2 = ((f32[16,16,128]{2,1,0:T(8,128)}), f32[16,16,128]{2,1,0:T(8,128)S(1)}, u32[]{:S(2)}, u32[]{:S(2)}) async-start(f32[16,16,128]{2,1,0:T(8,128)} %broadcast_in_dim.16), calls=%async_computation.2 | async-start | bytes 262144 | tf_op jit(solution)/shard_map/all_to_all | solution.py:26
  81.7 19.2 %all-to-all-start.3 = ((f32[16,144,128]{2,1,0:T(8,128)}), f32[16,144,128]{2,1,0:T(8,128)S(1)}, u32[]{:S(2)}, u32[]{:S(2)}) async-start(f32[16,144,128]{2,1,0:T(8,128)} %broadcast_dynamic-update-slice_fusion), calls=%async_computation.3 | async-start | bytes 2359296 | tf_op jit(solution)/shard_map/all_to_all | solution.py:207

commit v4 on v3

--- a/solution.py
+++ b/solution.py
@@ -14,7 +14,8 @@
 STEP = 8
 CHUNKS = 4
 VMEM = pl.BlockSpec(memory_space=pltpu.VMEM)
-ANY = pl.BlockSpec(memory_space=pl.ANY)
+HBM = pl.BlockSpec(memory_space=pltpu.HBM)
+FULL = pltpu.CompilerParams(vmem_limit_bytes=55_800_000)
 LIMIT = pltpu.CompilerParams(vmem_limit_bytes=32 << 20)
 
 
@@ -52,7 +53,7 @@
     return jnp.concatenate([block[:half], block[half:]], 1)
 
 
-def project(bt_ref, st_ref, out_ref, b_buf, s_buf, sems):
+def project(bt_ref, st_ref, coeffs_ref, pieces_ref, own_ref, b_buf, s_buf, sems):
     step = b_buf.shape[1] // CHUNKS
     copies = []
     for i in range(CHUNKS):
@@ -61,26 +62,67 @@
             copy = pltpu.make_async_copy(src.at[:, cut], dst.at[:, cut], sems.at[2 * i + k])
             copy.start()
             copies.append(copy)
+    part = pieces_ref.shape[2]
+    each = step // part
     total = None
     for i in range(CHUNKS):
         copies[2 * i].wait()
         copies[2 * i + 1].wait()
         cut = slice(i * step, (i + 1) * step)
-        term = dot3(b_buf[:, cut], s_buf[:, cut], 1, 1)
+        basis = b_buf[:, cut]
+        term = dot3(basis, s_buf[:, cut], 1, 1)
         total = term if total is None else total + term
-    out_ref[...] = pack(total)
-
-
-def remainder(got_ref, st_ref, resid_ref, gram_ref):
+        for j in range(each):
+            pieces_ref[i * each + j] = basis[:, j * part : (j + 1) * part]
+    coeffs_ref[...] = pack(total)
+    place = lax.axis_index("y") * lax.axis_size("x") + lax.axis_index("x")
+    own_ref[...] = s_buf[:, pl.ds(pl.multiple_of(place * part, part), part)]
+
+
+def share(both_ref, out_ref):
+    half = out_ref.shape[1]
+    both = both_ref[0] + both_ref[1]
+    mine = jnp.where(lax.axis_index(CORE) == 0, both[:half], both[half:])
+    for k in range(out_ref.shape[0]):
+        out_ref[k] = mine
+
+
+def added(ref):
+    total = ref[0]
+    for k in range(1, ref.shape[0]):
+        total = total + ref[k]
+    return total
+
+
+def bundle(coeffs_ref, pieces_ref, out_ref):
+    width = pieces_ref.shape[1]
+    out_ref[:, :width] = pieces_ref[...]
+    coeffs = added(coeffs_ref)
+    for j in range(out_ref.shape[0]):
+        out_ref[j, width:] = coeffs
+
+
+def bundle_back(gram_ref, rotated_ref, resid_ref, cols_ref, out_ref, cols_out_ref):
+    width, count = rotated_ref.shape[1], resid_ref.shape[0]
+    out_ref[:, :width] = rotated_ref[...]
+    gram, resid = added(gram_ref), resid_ref[...]
+    for j in range(out_ref.shape[0]):
+        out_ref[j, width : width + count] = resid
+        out_ref[j, width + count :] = gram
+    cols_out_ref[...] = cols_ref[...]
+
+
+def remainder(got_ref, coeffs_ref, st_ref, resid_ref, gram_ref):
     modes, _, part = got_ref.shape
+    cores, _, few, _ = coeffs_ref.shape
     count = st_ref.shape[0]
-    width = got_ref.shape[1] - count // 2
-    half = width // 2
-    got = got_ref[...]
-    upper = got[:, :half].reshape(modes * half, part)
-    lower = got[:, half:width].reshape(modes * half, part)
-    coeffs = got[:, width:].reshape(modes * half, 2 * count)
-    both = dot3(coeffs.T, jnp.concatenate([upper, lower], 1))
+
+    def stack(first):
+        cuts = [got_ref[:, first + c * few : first + (c + 1) * few] for c in range(cores)]
+        return jnp.concatenate([cut.reshape(modes * few, part) for cut in cuts], 0)
+
+    coeffs = coeffs_ref[...].reshape(cores * modes * few, 2 * count)
+    both = dot3(coeffs.T, jnp.concatenate([stack(0), stack(cores * few)], 1))
     resid = st_ref[...] - (both[:count, :part] + both[count:, part:])
     resid_ref[...] = resid
     gram_ref[...] = pack(dot3(resid, resid, 1, 1))
@@ -149,10 +191,23 @@
         )
 
 
-def core_half(block):
-    both = lax.all_gather(block, CORE, axis=0, tiled=False).sum(0)
-    half = both.shape[0] // 2
-    return lax.dynamic_slice_in_dim(both, lax.axis_index(CORE) * half, half, 0)
+def kernel(body, out, args, specs=None, scratch=(), params=LIMIT):
+    return pl.pallas_call(
+        body,
+        out_shape=out,
+        in_specs=specs or [VMEM] * len(args),
+        out_specs=(VMEM,) * len(out) if isinstance(out, tuple) else VMEM,
+        scratch_shapes=scratch,
+        compiler_params=params,
+    )(*args)
+
+
+def over_space(block, depth):
+    both = lax.all_gather(block, CORE, axis=0, tiled=False)
+    few = block.shape[0] // 2
+    return lax.all_to_all(
+        kernel(share, struct(depth, few, block.shape[1]), (both,)), Z, 0, 0, tiled=True
+    )
 
 
 def local(basis, snapshots, rotation):
@@ -161,60 +216,49 @@
     rows, width = basis.shape
     count = snapshots.shape[1]
     part = rows // modes
+    few = width // 4
     total = rotation.shape[1]
     place = lax.axis_index(MODE)
     scale = float(rows * depth * 2) ** 0.5
     bt, st = basis.T, snapshots.T
-    coeffs = pl.pallas_call(
+    buffers = (
+        pltpu.VMEM((width, rows), jnp.float32),
+        pltpu.VMEM((count, rows), jnp.float32),
+        pltpu.SemaphoreType.DMA((2 * CHUNKS,)),
+    )
+    coeffs, pieces, st_own = kernel(
         project,
-        out_shape=struct(width // 2, 2 * count),
-        in_specs=[ANY, ANY],
-        out_specs=VMEM,
-        scratch_shapes=[
-            pltpu.VMEM((width, rows), jnp.float32),
-            pltpu.VMEM((count, rows), jnp.float32),
-            pltpu.SemaphoreType.DMA((2 * CHUNKS,)),
-        ],
-        compiler_params=LIMIT,
-        name="project",
-    )(bt, st)
-    coeffs = spread(core_half(coeffs), Z, depth).sum(0)
-    coeffs = lax.all_gather(coeffs, CORE, axis=0, tiled=True)
-    pieces = bt.reshape(width, modes, part).transpose(1, 0, 2)
-    pieces = jnp.concatenate([pieces, jnp.zeros((modes, width // 2, part), jnp.float32)], 1)
-    pieces = lax.dynamic_update_slice(
-        pieces, jnp.broadcast_to(coeffs[None], (modes,) + coeffs.shape), (0, width, 0)
-    )
-    got = lax.all_to_all(pieces, MODE, 0, 0, tiled=True)
-    resid, gram = pl.pallas_call(
+        (struct(width // 2, 2 * count), struct(modes, width, part), struct(count, part)),
+        (bt, st),
+        [HBM, HBM],
+        buffers,
+        FULL,
+    )
+    coeffs = over_space(coeffs, depth)
+    got = kernel(bundle, struct(modes, width + few, part), (coeffs, pieces))
+    got = lax.all_to_all(got, MODE, 0, 0, tiled=True)
+    coeffs = lax.all_gather(got[:, width:], CORE, axis=0, tiled=False)
+    resid, gram = kernel(
         remainder,
-        out_shape=(struct(count, part), struct(count // 2, 2 * count)),
-        in_specs=[VMEM, VMEM],
-        out_specs=(VMEM, VMEM),
-        compiler_params=LIMIT,
-        name="remainder",
-    )(got, lax.dynamic_slice_in_dim(st, place * part, part, 1))
-    gram = spread(core_half(gram), Z, depth).sum(0)
+        (struct(count, part), struct(count // 2, 2 * count)),
+        (got, coeffs, st_own),
+    )
+    gram = over_space(gram, depth)
     own = got[:, :width].reshape(total, part)
     rotated = dot(rotation[:total], own, 0, 0).reshape(modes, width, part)
-    resid = jnp.broadcast_to(resid[None], (modes,) + resid.shape)
-    empty = jnp.zeros((modes,) + gram.shape, jnp.float32)
-    pieces = lax.dynamic_update_slice(
-        jnp.concatenate([rotated, resid, empty], 1),
-        jnp.broadcast_to(gram[None], (modes,) + gram.shape),
-        (0, width + count, 0),
+    lower_cols = lax.dynamic_slice(rotation, (total, place * width), (count, width))
+    pieces, lower_cols = kernel(
+        bundle_back,
+        (struct(modes, width + count + few, part), struct(count, width)),
+        (gram, rotated, resid, lower_cols),
     )
     parts = lax.all_to_all(pieces, MODE, 0, 0, tiled=True)
     gram = lax.all_gather(parts[:, width + count :].sum(0), CORE, axis=0, tiled=True)
-    lower_cols = lax.dynamic_slice(rotation, (total, place * width), (count, width))
-    out, factor = pl.pallas_call(
+    out, factor = kernel(
         functools.partial(finish, scale),
-        out_shape=(struct(width, rows), struct(count, count)),
-        in_specs=[VMEM] * 3,
-        out_specs=(VMEM, VMEM),
-        compiler_params=LIMIT,
-        name="finish",
-    )(gram, lower_cols, parts)
+        (struct(width, rows), struct(count, count)),
+        (gram, lower_cols, parts),
+    )
     return out.T, factor
 
 

time: 111 us -> 104 us (0.937)
  blocking collectives: 22.4 us -> 78.1 us
  waiting for transfers between devices: 46.7 us -> 7.47 us
  starting transfers between devices: 23.8 us -> 6.02 us
  local copies, waits for them, and re-layouts: 6.06 us -> 1.09 us
  other arithmetic: 2.16 us -> 0.02 us
  Pallas kernels: 4.76 us -> 6.38 us
    all_to_all x0 -> x3, blocking collectives: none -> 55.5 us  [the longest x1 21.5 us: over_space(): lax.all_to_all(kernel(share, struct(depth, few, block.shape[1]), (both,))...]
    all_to_all x4 -> x1, waiting for transfers between devices: 46.7 us -> 7.47 us  [over_space(): lax.all_to_all(kernel(share, struct(depth, few, block.shape[1]), (both,))...]
    all_to_all x4 -> x1, starting transfers between devices: 23.8 us -> 6.02 us  [over_space(): lax.all_to_all(kernel(share, struct(depth, few, block.shape[1]), (both,))...]
    unnamed x6 -> x0, local copies, waits for them, and re-layouts: 2.08 us -> none
    pallas_call x3 -> x7, Pallas kernels: 4.76 us -> 6.38 us  [kernel(): pl.pallas_call(body, out_shape=out, in_specs=specs or [VMEM] * len(args),...]
    broadcast_in_dim x5 -> x0, local copies, waits for them, and re-layouts: 1.4 us -> none  [the longest x2 1.33 us: spread(): jnp.broadcast_to(block[None], (count,) + block.shape)]
    concatenate x1 -> x0, other arithmetic: 1.16 us -> none  [local(): jnp.concatenate([rotated, resid, empty], 1)]
  transfers between devices with their start and end apart: 4 -> 1, of which waited for: 4 -> 1; matrix products, arithmetic and copies ran while one was open for 6% -> 4% of each run, Pallas kernels for 0% -> 0%
where the time goes in v4:
time: 104 us; the launch traced here: 103 us
  blocking collectives  78.1 us (75%)
  waiting for transfers between devices  7.47 us (7%)
  Pallas kernels  6.38 us (6%)
  starting transfers between devices  6.02 us (6%)
  matrix products  3.55 us (3%)
  local copies, waits for them, and re-layouts  1.09 us (1%)
    all_to_all x1, blocking collectives, over_space(): lax.all_to_all(kernel(share, struct(depth, few, block.shape[1]), (both,))...  21.5 us
    all_to_all x1, blocking collectives, local(): parts = lax.all_to_all(pieces, MODE, 0, 0, tiled=True)  17.7 us
    all_to_all x1, blocking collectives, local(): got = lax.all_to_all(got, MODE, 0, 0, tiled=True)  16.3 us
    all_gather x2, blocking collectives, over_space(): both = lax.all_gather(block, CORE, axis=0, tiled=False)  10.3 us
    all_to_all x1, waiting for transfers between devices, over_space(): lax.all_to_all(kernel(share, struct(depth, few, block.shape[1]), (both,))...  7.47 us
    pallas_call x7, Pallas kernels, kernel(): pl.pallas_call(body, out_shape=out, in_specs=specs or [VMEM] * len(args),...  6.38 us
    all_gather x1, blocking collectives, local(): coeffs = lax.all_gather(got[:, width:], CORE, axis=0, tiled=False)  6.18 us
    all_gather x1, blocking collectives, local(): lax.all_gather(parts[:, width + count:].sum(0), CORE, axis=0, tiled=True)  6.16 us
  transfers between devices with their start and end apart: 1, of which 1 were waited for; matrix products, arithmetic and copies ran while one was open for 4% of the time, Pallas kernels for 0%

profile of v4, /device:TPU:1, one launch (start us, length us, event | category | flops | bytes accessed | tf_op | source)
XLA Modules:
  0.0 103.4 jit_solution(10730683531647314960)
XLA Ops:
  0.6 1.8 %shard_map.50 = (f32[32,128]{1,0:T(8,128)S(1)}, f32[16,64,128]{2,1,0:T(8,128)S(1)}, f32[64,128]{1,0:T(8,128)S(1)}) custom-call(f32[64,2048]{1,0:T(8,128)} %bitcast.16, f32[64,2048]{1,0:T(8,128)} %bitcast.17), custom_call_target="tpu_custom_call" | custom-call | tf_op jit(solution)/shard_map/pallas_call | solution.py:195
  2.5 8.4 %all-gather = f32[64,128]{1,0:T(8,128)S(1)} all-gather(f32[32,128]{1,0:T(8,128)S(1)} %get-tuple-element.11), channel_id=2, replica_groups=mesh['z'=16,'core'=2,'y'=4,'x'=4] {'core'}, dimensions={0}, use_global_device_ids=true | all-gather | bytes 49152 | tf_op jit(solution)/shard_map/all_gather | solution.py:206
  10.9 21.5 %all_to_all.20.coeffs_ref = f32[16,16,128]{2,1,0:T(8,128)S(1)} all-to-all(f32[16,16,128]{2,1,0:T(8,128)S(1)} %shard_map.51), channel_id=1, replica_groups=mesh['z'=16,'core'=2,'y'=4,'x'=4] {'z'}, dimensions={0} | all-to-all | bytes 262144 | tf_op jit(solution)/shard_map/all_to_all | solution.py:208
  32.3 0.1 shard_map.52
  32.4 16.3 %all_to_all.21.got_ref = f32[16,80,128]{2,1,0:T(8,128)S(1)} all-to-all(f32[16,80,128]{2,1,0:T(8,128)S(1)} %shard_map.52), channel_id=1, replica_groups=mesh['z'=16,'core'=2,'y'=4,'x'=4] {'y','x'}, dimensions={0} | all-to-all | bytes 1310720 | tf_op jit(solution)/shard_map/all_to_all | solution.py:239
  48.8 6.2 %all-gather.1 = f32[32,16,128]{2,1,0:T(8,128)S(1)} all-gather(f32[16,16,128]{2,1,0:T(8,128)S(1)} %slice.16), channel_id=3, replica_groups=mesh['z'=16,'core'=2,'y'=4,'x'=4] {'core'}, dimensions={0}, use_global_device_ids=true | all-gather | bytes 393216 | tf_op jit(solution)/shard_map/all_gather | solution.py:240
  54.9 0.5 shard_map.53
  55.5 1.9 %all-gather.2 = f32[64,128]{1,0:T(8,128)S(1)} all-gather(f32[32,128]{1,0:T(8,128)S(1)} %get-tuple-element.14), channel_id=4, replica_groups=mesh['z'=16,'core'=2,'y'=4,'x'=4] {'core'}, dimensions={0}, use_global_device_ids=true | all-gather | bytes 49152 | tf_op jit(solution)/shard_map/all_gather | solution.py:206
  57.4 0.7 shard_map.54
  58.0 6.0 %all-to-all-start.2 = ((f32[16,16,128]{2,1,0:T(8,128)}), f32[16,16,128]{2,1,0:T(8,128)S(1)}, u32[]{:S(2)}, u32[]{:S(2)}) async-start(f32[16,16,128]{2,1,0:T(8,128)} %shard_map.54), calls=%async_computation.2 | async-start | bytes 262144 | tf_op jit(solution)/shard_map/all_to_all | solution.py:208
  64.1 0.8 constant_dynamic-slice_fusion.cols_ref
  64.9 0.1 slice.17
  65.0 3.6 %fusion.2 = f32[1024,128]{0,1:T(8,128)S(1)} fusion(f32[1024,128]{1,0:T(8,128)S(1)} %bitcast.15, f32[1088,1024]{1,0:T(8,128)} %param.5), kind=kOutput, calls=%fused_computation.2 | convolution fusion | flops 805306368 | bytes 5242880 | tf_op jit(solution)/shard_map/dot_general | solution.py:33
  68.5 0.2 copy.6
  68.7 7.5 %all-to-all-done.2.gram_ref = f32[16,16,128]{2,1,0:T(8,128)S(1)} async-done(((f32[16,16,128]{2,1,0:T(8,128)}), f32[16,16,128]{2,1,0:T(8,128)S(1)}, u32[]{:S(2)}, u32[]{:S(2)}) %all-to-all-start.2) | async-done | bytes 131104 | tf_op jit(solution)/shard_map/all_to_all | solution.py:208
  76.2 0.1 shard_map.55
  76.3 17.7 %all_to_all.22.parts_ref = f32[16,144,128]{2,1,0:T(8,128)S(1)} all-to-all(f32[16,144,128]{2,1,0:T(8,128)S(1)} %get-tuple-element.16), channel_id=1, replica_groups=mesh['z'=16,'core'=2,'y'=4,'x'=4] {'y','x'}, dimensions={0} | all-to-all | bytes 2359296 | tf_op jit(solution)/shard_map/all_to_all | solution.py:255
  94.0 6.2 %all_gather.27.gram_ref = f32[32,128]{1,0:T(8,128)S(1)} all-gather(f32[16,128]{1,0:T(8,128)S(1)} %slice_reduce_fusion), channel_id=1, replica_groups=mesh['z'=16,'core'=2,'y'=4,'x'=4] {'core'}, dimensions={0}, use_global_device_ids=true | all-gather | bytes 24576 | tf_op jit(solution)/shard_map/all_gather | solution.py:256
  100.1 3.2 %shard_map.56 = (f32[64,2048]{1,0:T(8,128)}, f32[64,64]{1,0:T(8,128)}) custom-call(f32[32,128]{1,0:T(8,128)S(1)} %all_gather.27.gram_ref, f32[64,64]{1,0:T(8,128)S(1)} %get-tuple-element.17.lower_cols_ref, f32[16,144,128]{2,1,0:T(8,128)S(1)} %all_to_all.22.parts_ref), custom_call_target="tpu_custom_call" | custom-call | tf_op jit(solution)/shard_map/pallas_call | solution.py:195
  (3 shorter events, 0.0 us)
Async XLA Ops:
  58.0 18.2 %all-to-all-start.2 = ((f32[16,16,128]{2,1,0:T(8,128)}), f32[16,16,128]{2,1,0:T(8,128)S(1)}, u32[]{:S(2)}, u32[]{:S(2)}) async-start(f32[16,16,128]{2,1,0:T(8,128)} %shard_map.54), calls=%async_computation.2 | async-start | bytes 262144 | tf_op jit(solution)/shard_map/all_to_all | solution.py:208

commit v5 on v4

--- a/solution.py
+++ b/solution.py
@@ -2,6 +2,7 @@
 
 import jax
 import jax.numpy as jnp
+import numpy as np
 from jax import lax
 from jax.experimental import pallas as pl
 from jax.experimental.pallas import tpu as pltpu
@@ -23,12 +24,6 @@
     return jax.ShapeDtypeStruct(shape, jnp.float32)
 
 
-def spread(block, axes, count):
-    return lax.all_to_all(
-        jnp.broadcast_to(block[None], (count,) + block.shape), axes, 0, 0, tiled=True
-    )
-
-
 def dot(a, b, left, right):
     return lax.dot_general(a, b, (((left,), (right,)), ((), ())), precision=HIGH)
 
@@ -53,7 +48,7 @@
     return jnp.concatenate([block[:half], block[half:]], 1)
 
 
-def project(bt_ref, st_ref, coeffs_ref, pieces_ref, own_ref, b_buf, s_buf, sems):
+def project(bt_ref, st_ref, first_ref, pieces_ref, own_ref, b_buf, s_buf, sems):
     step = b_buf.shape[1] // CHUNKS
     copies = []
     for i in range(CHUNKS):
@@ -62,8 +57,8 @@
             copy = pltpu.make_async_copy(src.at[:, cut], dst.at[:, cut], sems.at[2 * i + k])
             copy.start()
             copies.append(copy)
-    part = pieces_ref.shape[2]
-    each = step // part
+    _, width, part = pieces_ref.shape
+    each, half = step // part, width // 2
     total = None
     for i in range(CHUNKS):
         copies[2 * i].wait()
@@ -72,17 +67,31 @@
         basis = b_buf[:, cut]
         term = dot3(basis, s_buf[:, cut], 1, 1)
         total = term if total is None else total + term
-        for j in range(each):
-            pieces_ref[i * each + j] = basis[:, j * part : (j + 1) * part]
-    coeffs_ref[...] = pack(total)
+        for j in range(i * each, (i + 1) * each):
+            piece = b_buf[:, j * part : (j + 1) * part]
+            pieces_ref[j] = piece
+            first_ref[(j + 1) * half : (j + 2) * half] = piece[half:]
+    first_ref[:half] = pack(total)
     place = lax.axis_index("y") * lax.axis_size("x") + lax.axis_index("x")
     own_ref[...] = s_buf[:, pl.ds(pl.multiple_of(place * part, part), part)]
 
 
+def first_core():
+    return lax.axis_index(CORE) == 0
+
+
 def share(both_ref, out_ref):
+    count, half, _ = out_ref.shape
+    coeffs = both_ref[0, :half] + both_ref[1, :half]
+    for k in range(count):
+        piece = both_ref[1, (k + 1) * half : (k + 2) * half]
+        out_ref[k] = jnp.where(first_core(), piece, coeffs)
+
+
+def share_back(both_ref, out_ref):
     half = out_ref.shape[1]
-    both = both_ref[0] + both_ref[1]
-    mine = jnp.where(lax.axis_index(CORE) == 0, both[:half], both[half:])
+    gram = both_ref[0, :half] + both_ref[1, :half]
+    mine = jnp.where(first_core(), both_ref[1, half:], gram)
     for k in range(out_ref.shape[0]):
         out_ref[k] = mine
 
@@ -94,38 +103,54 @@
     return total
 
 
-def bundle(coeffs_ref, pieces_ref, out_ref):
-    width = pieces_ref.shape[1]
-    out_ref[:, :width] = pieces_ref[...]
-    coeffs = added(coeffs_ref)
+def bundle(crossed_ref, pieces_ref, out_ref):
+    half = crossed_ref.shape[1]
+    coeffs = added(crossed_ref)
+    out_ref[:, :half] = pieces_ref[:, :half]
     for j in range(out_ref.shape[0]):
-        out_ref[j, width:] = coeffs
-
-
-def bundle_back(gram_ref, rotated_ref, resid_ref, cols_ref, out_ref, cols_out_ref):
-    width, count = rotated_ref.shape[1], resid_ref.shape[0]
+        out_ref[j, half:] = jnp.where(first_core(), pieces_ref[j, half:], coeffs)
+
+
+def trade(crossed_ref, got_ref, out_ref):
+    half = crossed_ref.shape[1]
+    out_ref[...] = jnp.where(first_core(), crossed_ref[...], got_ref[:, half:])
+
+
+def remainder(got_ref, traded_ref, st_ref, resid_ref, both_ref):
+    modes, width, part = got_ref.shape
+    count = st_ref.shape[0]
+    half = width // 2
+    lower = got_ref[:, :half]
+    upper = jnp.where(first_core(), got_ref[:, half:], traded_ref[0])
+    rows = [block.reshape(modes * half, part) for block in (lower, upper)]
+    coeffs = traded_ref[1].reshape(modes * half, 2 * count)
+    back = dot3(coeffs.T, jnp.concatenate(rows, 1))
+    resid = st_ref[...] - (back[:count, :part] + back[count:, part:])
+    resid_ref[...] = resid
+    both_ref[: count // 2] = pack(dot3(resid, resid, 1, 1))
+    both_ref[count // 2 :] = resid[count // 2 :]
+
+
+def bundle_back(crossed_ref, rotated_ref, resid_ref, cols_ref, out_ref, cols_out_ref):
+    width, half = rotated_ref.shape[1], crossed_ref.shape[1]
+    gram = added(crossed_ref)
     out_ref[:, :width] = rotated_ref[...]
-    gram, resid = added(gram_ref), resid_ref[...]
+    early = resid_ref[:half]
+    late = jnp.where(first_core(), resid_ref[half:], gram)
     for j in range(out_ref.shape[0]):
-        out_ref[j, width : width + count] = resid
-        out_ref[j, width + count :] = gram
+        out_ref[j, width : width + half] = early
+        out_ref[j, width + half :] = late
     cols_out_ref[...] = cols_ref[...]
 
 
-def remainder(got_ref, coeffs_ref, st_ref, resid_ref, gram_ref):
-    modes, _, part = got_ref.shape
-    cores, _, few, _ = coeffs_ref.shape
-    count = st_ref.shape[0]
-
-    def stack(first):
-        cuts = [got_ref[:, first + c * few : first + (c + 1) * few] for c in range(cores)]
-        return jnp.concatenate([cut.reshape(modes * few, part) for cut in cuts], 0)
-
-    coeffs = coeffs_ref[...].reshape(cores * modes * few, 2 * count)
-    both = dot3(coeffs.T, jnp.concatenate([stack(0), stack(cores * few)], 1))
-    resid = st_ref[...] - (both[:count, :part] + both[count:, part:])
-    resid_ref[...] = resid
-    gram_ref[...] = pack(dot3(resid, resid, 1, 1))
+def last(crossed_ref, parts_ref, out_ref):
+    modes, half, part = crossed_ref.shape
+    out_ref[: modes * half] = crossed_ref[...].reshape(modes * half, part)
+    start = parts_ref.shape[1] - half
+    total = parts_ref[0, start:]
+    for j in range(1, modes):
+        total = total + parts_ref[j, start:]
+    out_ref[modes * half :] = total
 
 
 def eliminate(gram):
@@ -177,18 +202,21 @@
     return jnp.concatenate(done, 0)
 
 
-def finish(scale, gram_ref, lower_cols_ref, parts_ref, out_ref, factor_ref):
-    count = lower_cols_ref.shape[0]
-    packed = gram_ref[...]
+def finish(scale, last_ref, lower_cols_ref, parts_ref, out_ref, factor_ref):
+    count, width = lower_cols_ref.shape
+    half = count // 2
+    modes, _, part = parts_ref.shape
+    packed = last_ref[1, modes * half :]
     done = eliminate(jnp.concatenate([packed[:, :count], packed[:, count:]], 0))
     factor_ref[...] = done[:, :count].T * (1.0 / scale)
     weights = dot3(lower_cols_ref[...].T, done[:, count:]) * scale
-    modes, _, part = parts_ref.shape
     for j in range(modes):
-        piece = parts_ref[j]
-        out_ref[:, j * part : (j + 1) * part] = piece[:count] * scale + dot3(
-            weights, piece[count : 2 * count]
+        early = parts_ref[j, width : width + half]
+        late = jnp.where(
+            first_core(), parts_ref[j, width + half :], last_ref[0, j * half : (j + 1) * half]
         )
+        resid = jnp.concatenate([early, late], 0)
+        out_ref[:, j * part : (j + 1) * part] = parts_ref[j, :width] * scale + dot3(weights, resid)
 
 
 def kernel(body, out, args, specs=None, scratch=(), params=LIMIT):
@@ -210,13 +238,29 @@
     )
 
 
+def cross(block, depth, modes):
+    devices = np.arange(2 * depth * modes).reshape(depth, 2, modes)
+    groups = devices[:, 1].T.tolist() + devices[:, 0].tolist()
+    return lax.all_to_all(
+        block, (Z, CORE) + MODE, 0, 0, tiled=True, axis_index_groups=groups
+    )
+
+
+def over_cores(block):
+    return lax.all_gather(block, CORE, axis=0, tiled=False)
+
+
+def over_mode(block):
+    return lax.all_to_all(block, MODE, 0, 0, tiled=True)
+
+
 def local(basis, snapshots, rotation):
     depth = lax.axis_size(Z)
     modes = lax.axis_size("y") * lax.axis_size("x")
     rows, width = basis.shape
     count = snapshots.shape[1]
     part = rows // modes
-    few = width // 4
+    half = width // 2
     total = rotation.shape[1]
     place = lax.axis_index(MODE)
     scale = float(rows * depth * 2) ** 0.5
@@ -226,38 +270,38 @@
         pltpu.VMEM((count, rows), jnp.float32),
         pltpu.SemaphoreType.DMA((2 * CHUNKS,)),
     )
-    coeffs, pieces, st_own = kernel(
+    first, pieces, st_own = kernel(
         project,
-        (struct(width // 2, 2 * count), struct(modes, width, part), struct(count, part)),
+        (struct((modes + 1) * half, part), struct(modes, width, part), struct(count, part)),
         (bt, st),
         [HBM, HBM],
         buffers,
         FULL,
     )
-    coeffs = over_space(coeffs, depth)
-    got = kernel(bundle, struct(modes, width + few, part), (coeffs, pieces))
-    got = lax.all_to_all(got, MODE, 0, 0, tiled=True)
-    coeffs = lax.all_gather(got[:, width:], CORE, axis=0, tiled=False)
-    resid, gram = kernel(
-        remainder,
-        (struct(count, part), struct(count // 2, 2 * count)),
-        (got, coeffs, st_own),
-    )
-    gram = over_space(gram, depth)
-    own = got[:, :width].reshape(total, part)
+    crossed = kernel(share, struct(depth, half, part), (over_cores(first),))
+    crossed = cross(crossed, depth, modes)
+    got = over_mode(kernel(bundle, struct(modes, width, part), (crossed, pieces)))
+    traded = over_cores(kernel(trade, struct(modes, half, part), (crossed, got)))
+    resid, both = kernel(
+        remainder, (struct(count, part), struct(2 * half, part)), (got, traded, st_own)
+    )
+    crossed = kernel(share_back, struct(depth, half, part), (over_cores(both),))
+    crossed = cross(crossed, depth, modes)
+    later = jnp.where(lax.axis_index(CORE) == 0, got[:, half:], traded[0])
+    own = jnp.concatenate([got[:, :half], later], 1).reshape(total, part)
     rotated = dot(rotation[:total], own, 0, 0).reshape(modes, width, part)
     lower_cols = lax.dynamic_slice(rotation, (total, place * width), (count, width))
     pieces, lower_cols = kernel(
         bundle_back,
-        (struct(modes, width + count + few, part), struct(count, width)),
-        (gram, rotated, resid, lower_cols),
-    )
-    parts = lax.all_to_all(pieces, MODE, 0, 0, tiled=True)
-    gram = lax.all_gather(parts[:, width + count :].sum(0), CORE, axis=0, tiled=True)
+        (struct(modes, width + count, part), struct(count, width)),
+        (crossed, rotated, resid, lower_cols),
+    )
+    parts = over_mode(pieces)
+    gathered = over_cores(kernel(last, struct((modes + 1) * half, part), (crossed, parts)))
     out, factor = kernel(
         functools.partial(finish, scale),
         (struct(width, rows), struct(count, count)),
-        (gram, lower_cols, parts),
+        (gathered, lower_cols, parts),
     )
     return out.T, factor
 

time: 104 us -> 95.5 us (0.918)
  blocking collectives: 78.1 us -> 67.4 us
    all_gather x4, blocking collectives: 22.6 us -> 15 us  [over_cores(): return lax.all_gather(block, CORE, axis=0, tiled=False)]
    all_to_all x3, blocking collectives: 55.5 us -> 52.4 us  [the longest x2 30.3 us: over_mode(): return lax.all_to_all(block, MODE, 0, 0, tiled=True)]
    unnamed x0 -> x2, local copies, waits for them, and re-layouts: none -> 1.04 us
    pallas_call x7 -> x9, Pallas kernels: 6.38 us -> 7.04 us  [kernel(): pl.pallas_call(body, out_shape=out, in_specs=specs or [VMEM] * len(args),...]
  transfers between devices with their start and end apart: 1 -> 1, of which waited for: 1 -> 1; matrix products, arithmetic and copies ran while one was open for 4% -> 5% of each run, Pallas kernels for 0% -> 0%
where the time goes in v5:
time: 95.5 us; the launch traced here: 94.7 us
  blocking collectives  67.4 us (71%)
  waiting for transfers between devices  8.14 us (9%)
  Pallas kernels  7.04 us (7%)
  starting transfers between devices  5.74 us (6%)
  matrix products  3.47 us (4%)
  local copies, waits for them, and re-layouts  2.08 us (2%)
    all_to_all x2, blocking collectives, over_mode(): return lax.all_to_all(block, MODE, 0, 0, tiled=True)  30.3 us
    all_to_all x1, blocking collectives, cross(): lax.all_to_all(block, (Z, CORE) + MODE, 0, 0, tiled=True, axis_index_grou...  22.1 us
    all_gather x4, blocking collectives, over_cores(): return lax.all_gather(block, CORE, axis=0, tiled=False)  15 us
    all_to_all x1, waiting for transfers between devices, cross(): lax.all_to_all(block, (Z, CORE) + MODE, 0, 0, tiled=True, axis_index_grou...  8.14 us
    pallas_call x9, Pallas kernels, kernel(): pl.pallas_call(body, out_shape=out, in_specs=specs or [VMEM] * len(args),...  7.04 us
    all_to_all x1, starting transfers between devices, cross(): lax.all_to_all(block, (Z, CORE) + MODE, 0, 0, tiled=True, axis_index_grou...  5.74 us
    dot_general x1, matrix products, dot(): lax.dot_general(a, b, (((left,), (right,)), ((), ())), precision=HIGH)  3.47 us
  transfers between devices with their start and end apart: 1, of which 1 were waited for; matrix products, arithmetic and copies ran while one was open for 5% of the time, Pallas kernels for 0%

profile of v5, /device:TPU:1, one launch (start us, length us, event | category | flops | bytes accessed | tf_op | source)
XLA Modules:
  0.0 94.7 jit_solution(14055884579441984103)
XLA Ops:
  0.6 2.4 %shard_map.50 = (f32[544,128]{1,0:T(8,128)S(1)}, f32[16,64,128]{2,1,0:T(8,128)}, f32[64,128]{1,0:T(8,128)S(1)}) custom-call(f32[64,2048]{1,0:T(8,128)} %bitcast.18, f32[64,2048]{1,0:T(8,128)} %bitcast.19), custom_call_target="tpu_custom_call" | custom-call | tf_op jit(solution)/shard_map/pallas_call | solution.py:223
  3.0 8.7 %all-gather = f32[1088,128]{1,0:T(8,128)S(1)} all-gather(f32[544,128]{1,0:T(8,128)S(1)} %get-tuple-element.11), channel_id=2, replica_groups=mesh['z'=16,'core'=2,'y'=4,'x'=4] {'core'}, dimensions={0}, use_global_device_ids=true | all-gather | bytes 835584 | tf_op jit(solution)/shard_map/all_gather | solution.py:250
  11.7 22.1 %all_to_all.20.crossed_ref = f32[16,32,128]{2,1,0:T(8,128)S(1)} all-to-all(f32[16,32,128]{2,1,0:T(8,128)S(1)} %shard_map.51), channel_id=1, replica_groups={{16,48,80,112,144,176,208,240,272,304,336,368,400,432,464,496},{17,49,8..., dimensions={0} | all-to-all | bytes 524288 | tf_op jit(solution)/shard_map/all_to_all | solution.py:244
  33.9 0.0 copy-start
  33.9 1.0 %copy-done = f32[16,64,128]{2,1,0:T(8,128)S(1)} copy-done((f32[16,64,128]{2,1,0:T(8,128)S(1)}, f32[16,64,128]{2,1,0:T(8,128)}, u32[]{:S(2)}) %copy-start) | copy-done | bytes 524312
  34.9 0.1 shard_map.52
  35.0 15.5 %all_to_all.21.got_ref = f32[16,64,128]{2,1,0:T(8,128)S(1)} all-to-all(f32[16,64,128]{2,1,0:T(8,128)S(1)} %shard_map.52), channel_id=1, replica_groups=mesh['z'=16,'core'=2,'y'=4,'x'=4] {'y','x'}, dimensions={0} | all-to-all | bytes 1048576 | tf_op jit(solution)/shard_map/all_to_all | solution.py:254
  50.5 2.2 %all-gather.1 = f32[32,32,128]{2,1,0:T(8,128)S(1)} all-gather(f32[16,32,128]{2,1,0:T(8,128)S(1)} %shard_map.53), channel_id=3, replica_groups=mesh['z'=16,'core'=2,'y'=4,'x'=4] {'core'}, dimensions={0}, use_global_device_ids=true | all-gather | bytes 786432 | tf_op jit(solution)/shard_map/all_gather | solution.py:250
  52.7 0.5 shard_map.54
  53.2 1.9 %all-gather.2 = f32[128,128]{1,0:T(8,128)S(1)} all-gather(f32[64,128]{1,0:T(8,128)S(1)} %get-tuple-element.14), channel_id=4, replica_groups=mesh['z'=16,'core'=2,'y'=4,'x'=4] {'core'}, dimensions={0}, use_global_device_ids=true | all-gather | bytes 98304 | tf_op jit(solution)/shard_map/all_gather | solution.py:250
  55.1 0.7 shard_map.55
  55.9 5.7 %all-to-all-start.2 = ((f32[16,32,128]{2,1,0:T(8,128)}), f32[16,32,128]{2,1,0:T(8,128)S(1)}, u32[]{:S(2)}, u32[]{:S(2)}) async-start(f32[16,32,128]{2,1,0:T(8,128)} %shard_map.55), calls=%async_computation.2 | async-start | bytes 524288 | tf_op jit(solution)/shard_map/all_to_all | solution.py:244
  61.6 0.8 constant_dynamic-slice_fusion.cols_ref
  62.5 0.1 fusion.5
  62.6 3.5 %fusion.2 = f32[1024,128]{0,1:T(8,128)S(1)} fusion(f32[1024,128]{1,0:T(8,128)S(1)} %bitcast.17, f32[1088,1024]{1,0:T(8,128)} %param.5), kind=kOutput, calls=%fused_computation.2 | convolution fusion | flops 805306368 | bytes 5242880 | tf_op jit(solution)/shard_map/dot_general | solution.py:28
  66.1 0.2 copy.6
  66.3 8.1 %all-to-all-done.2.crossed_ref = f32[16,32,128]{2,1,0:T(8,128)S(1)} async-done(((f32[16,32,128]{2,1,0:T(8,128)}), f32[16,32,128]{2,1,0:T(8,128)S(1)}, u32[]{:S(2)}, u32[]{:S(2)}) %all-to-all-start.2) | async-done | bytes 262176 | tf_op jit(solution)/shard_map/all_to_all | solution.py:244
  74.4 0.1 shard_map.56
  74.5 14.8 %all_to_all.22.parts_ref = f32[16,128,128]{2,1,0:T(8,128)S(1)} all-to-all(f32[16,128,128]{2,1,0:T(8,128)S(1)} %get-tuple-element.16), channel_id=1, replica_groups=mesh['z'=16,'core'=2,'y'=4,'x'=4] {'y','x'}, dimensions={0} | all-to-all | bytes 2097152 | tf_op jit(solution)/shard_map/all_to_all | solution.py:254
  89.3 2.2 %all-gather.3 = f32[1088,128]{1,0:T(8,128)S(1)} all-gather(f32[544,128]{1,0:T(8,128)S(1)} %shard_map.57), channel_id=5, replica_groups=mesh['z'=16,'core'=2,'y'=4,'x'=4] {'core'}, dimensions={0}, use_global_device_ids=true | all-gather | bytes 835584 | tf_op jit(solution)/shard_map/all_gather | solution.py:250
  91.5 3.2 %shard_map.58 = (f32[64,2048]{1,0:T(8,128)}, f32[64,64]{1,0:T(8,128)}) custom-call(f32[2,544,128]{2,1,0:T(8,128)S(1)} %bitcast.13, f32[64,64]{1,0:T(8,128)S(1)} %get-tuple-element.17.lower_cols_ref, f32[16,128,128]{2,1,0:T(8,128)S(1)} %all_to_all.22.parts_ref), custom_call_target="tpu_custom_call" | custom-call | tf_op jit(solution)/shard_map/pallas_call | solution.py:223
  (4 shorter events, 0.1 us)
Async XLA Ops:
  33.9 1.0 %copy-start = (f32[16,64,128]{2,1,0:T(8,128)S(1)}, f32[16,64,128]{2,1,0:T(8,128)}, u32[]{:S(2)}) copy-start(f32[16,64,128]{2,1,0:T(8,128)} %get-tuple-element.12.pieces_ref) | copy-start | bytes 1572868
  55.9 18.5 %all-to-all-start.2 = ((f32[16,32,128]{2,1,0:T(8,128)}), f32[16,32,128]{2,1,0:T(8,128)S(1)}, u32[]{:S(2)}, u32[]{:S(2)}) async-start(f32[16,32,128]{2,1,0:T(8,128)} %shard_map.55), calls=%async_computation.2 | async-start | bytes 524288 | tf_op jit(solution)/shard_map/all_to_all | solution.py:244

commit v6 on v5

--- a/solution.py
+++ b/solution.py
@@ -16,7 +16,7 @@
 CHUNKS = 4
 VMEM = pl.BlockSpec(memory_space=pltpu.VMEM)
 HBM = pl.BlockSpec(memory_space=pltpu.HBM)
-FULL = pltpu.CompilerParams(vmem_limit_bytes=55_800_000)
+FULL = pltpu.CompilerParams(vmem_limit_bytes=55_700_000)
 LIMIT = pltpu.CompilerParams(vmem_limit_bytes=32 << 20)
 
 
@@ -48,7 +48,33 @@
     return jnp.concatenate([block[:half], block[half:]], 1)
 
 
-def project(bt_ref, st_ref, first_ref, pieces_ref, own_ref, b_buf, s_buf, sems):
+def pack_symmetric(block):
+    half = block.shape[0] // 2
+    cut = 3 * half // 4
+    quarters = (block[:half, :half], block[half:, :half], block[half:, half:])
+    side = jnp.concatenate([quarter[cut:] for quarter in quarters], 0)
+    return jnp.concatenate([quarter[:cut] for quarter in quarters] + [side], 1)
+
+
+def unpack_symmetric(packed):
+    half = packed.shape[1] // 4
+    step = packed.shape[0] // 3
+    first, cross, second = (
+        jnp.concatenate(
+            [
+                packed[:, k * half : (k + 1) * half],
+                packed[k * step : (k + 1) * step, 3 * half :],
+            ],
+            0,
+        )
+        for k in range(3)
+    )
+    return jnp.concatenate(
+        [jnp.concatenate([first, cross.T], 1), jnp.concatenate([cross, second], 1)], 0
+    )
+
+
+def project(bt_ref, st_ref, first_ref, early_ref, own_ref, b_buf, s_buf, sems):
     step = b_buf.shape[1] // CHUNKS
     copies = []
     for i in range(CHUNKS):
@@ -57,8 +83,8 @@
             copy = pltpu.make_async_copy(src.at[:, cut], dst.at[:, cut], sems.at[2 * i + k])
             copy.start()
             copies.append(copy)
-    _, width, part = pieces_ref.shape
-    each, half = step // part, width // 2
+    _, half, part = early_ref.shape
+    each = step // part
     total = None
     for i in range(CHUNKS):
         copies[2 * i].wait()
@@ -69,7 +95,7 @@
         total = term if total is None else total + term
         for j in range(i * each, (i + 1) * each):
             piece = b_buf[:, j * part : (j + 1) * part]
-            pieces_ref[j] = piece
+            early_ref[j] = piece[:half]
             first_ref[(j + 1) * half : (j + 2) * half] = piece[half:]
     first_ref[:half] = pack(total)
     place = lax.axis_index("y") * lax.axis_size("x") + lax.axis_index("x")
@@ -89,9 +115,9 @@
 
 
 def share_back(both_ref, out_ref):
-    half = out_ref.shape[1]
-    gram = both_ref[0, :half] + both_ref[1, :half]
-    mine = jnp.where(first_core(), both_ref[1, half:], gram)
+    few = out_ref.shape[1]
+    gram = both_ref[0, :few] + both_ref[1, :few]
+    mine = jnp.where(first_core(), both_ref[1, few:], gram)
     for k in range(out_ref.shape[0]):
         out_ref[k] = mine
 
@@ -103,12 +129,13 @@
     return total
 
 
-def bundle(crossed_ref, pieces_ref, out_ref):
+def bundle(crossed_ref, first_ref, early_ref, out_ref):
     half = crossed_ref.shape[1]
     coeffs = added(crossed_ref)
-    out_ref[:, :half] = pieces_ref[:, :half]
+    out_ref[:, :half] = early_ref[...]
     for j in range(out_ref.shape[0]):
-        out_ref[j, half:] = jnp.where(first_core(), pieces_ref[j, half:], coeffs)
+        piece = first_ref[(j + 1) * half : (j + 2) * half]
+        out_ref[j, half:] = jnp.where(first_core(), piece, coeffs)
 
 
 def trade(crossed_ref, got_ref, out_ref):
@@ -127,30 +154,32 @@
     back = dot3(coeffs.T, jnp.concatenate(rows, 1))
     resid = st_ref[...] - (back[:count, :part] + back[count:, part:])
     resid_ref[...] = resid
-    both_ref[: count // 2] = pack(dot3(resid, resid, 1, 1))
-    both_ref[count // 2 :] = resid[count // 2 :]
+    few = both_ref.shape[0] // 2
+    both_ref[:few] = pack_symmetric(dot3(resid, resid, 1, 1))
+    both_ref[few:] = resid[count - few :]
 
 
 def bundle_back(crossed_ref, rotated_ref, resid_ref, cols_ref, out_ref, cols_out_ref):
-    width, half = rotated_ref.shape[1], crossed_ref.shape[1]
+    width, few = rotated_ref.shape[1], crossed_ref.shape[1]
     gram = added(crossed_ref)
     out_ref[:, :width] = rotated_ref[...]
-    early = resid_ref[:half]
-    late = jnp.where(first_core(), resid_ref[half:], gram)
+    cut = resid_ref.shape[0] - few
+    early = resid_ref[:cut]
+    late = jnp.where(first_core(), resid_ref[cut:], gram)
     for j in range(out_ref.shape[0]):
-        out_ref[j, width : width + half] = early
-        out_ref[j, width + half :] = late
+        out_ref[j, width : width + cut] = early
+        out_ref[j, width + cut :] = late
     cols_out_ref[...] = cols_ref[...]
 
 
 def last(crossed_ref, parts_ref, out_ref):
-    modes, half, part = crossed_ref.shape
-    out_ref[: modes * half] = crossed_ref[...].reshape(modes * half, part)
-    start = parts_ref.shape[1] - half
+    modes, few, part = crossed_ref.shape
+    out_ref[: modes * few] = crossed_ref[...].reshape(modes * few, part)
+    start = parts_ref.shape[1] - few
     total = parts_ref[0, start:]
     for j in range(1, modes):
         total = total + parts_ref[j, start:]
-    out_ref[modes * half :] = total
+    out_ref[modes * few :] = total
 
 
 def eliminate(gram):
@@ -204,18 +233,17 @@
 
 def finish(scale, last_ref, lower_cols_ref, parts_ref, out_ref, factor_ref):
     count, width = lower_cols_ref.shape
-    half = count // 2
     modes, _, part = parts_ref.shape
-    packed = last_ref[1, modes * half :]
-    done = eliminate(jnp.concatenate([packed[:, :count], packed[:, count:]], 0))
+    few = last_ref.shape[1] // (modes + 1)
+    cut = width + count - few
+    done = eliminate(unpack_symmetric(last_ref[1, modes * few :]))
     factor_ref[...] = done[:, :count].T * (1.0 / scale)
     weights = dot3(lower_cols_ref[...].T, done[:, count:]) * scale
     for j in range(modes):
-        early = parts_ref[j, width : width + half]
         late = jnp.where(
-            first_core(), parts_ref[j, width + half :], last_ref[0, j * half : (j + 1) * half]
+            first_core(), parts_ref[j, cut:], last_ref[0, j * few : (j + 1) * few]
         )
-        resid = jnp.concatenate([early, late], 0)
+        resid = jnp.concatenate([parts_ref[j, width:cut], late], 0)
         out_ref[:, j * part : (j + 1) * part] = parts_ref[j, :width] * scale + dot3(weights, resid)
 
 
@@ -261,6 +289,7 @@
     count = snapshots.shape[1]
     part = rows // modes
     half = width // 2
+    few = 3 * count // 8
     total = rotation.shape[1]
     place = lax.axis_index(MODE)
     scale = float(rows * depth * 2) ** 0.5
@@ -270,9 +299,9 @@
         pltpu.VMEM((count, rows), jnp.float32),
         pltpu.SemaphoreType.DMA((2 * CHUNKS,)),
     )
-    first, pieces, st_own = kernel(
+    first, early, st_own = kernel(
         project,
-        (struct((modes + 1) * half, part), struct(modes, width, part), struct(count, part)),
+        (struct((modes + 1) * half, part), struct(modes, half, part), struct(count, part)),
         (bt, st),
         [HBM, HBM],
         buffers,
@@ -280,12 +309,12 @@
     )
     crossed = kernel(share, struct(depth, half, part), (over_cores(first),))
     crossed = cross(crossed, depth, modes)
-    got = over_mode(kernel(bundle, struct(modes, width, part), (crossed, pieces)))
+    got = over_mode(kernel(bundle, struct(modes, width, part), (crossed, first, early)))
     traded = over_cores(kernel(trade, struct(modes, half, part), (crossed, got)))
     resid, both = kernel(
-        remainder, (struct(count, part), struct(2 * half, part)), (got, traded, st_own)
-    )
-    crossed = kernel(share_back, struct(depth, half, part), (over_cores(both),))
+        remainder, (struct(count, part), struct(2 * few, part)), (got, traded, st_own)
+    )
+    crossed = kernel(share_back, struct(depth, few, part), (over_cores(both),))
     crossed = cross(crossed, depth, modes)
     later = jnp.where(lax.axis_index(CORE) == 0, got[:, half:], traded[0])
     own = jnp.concatenate([got[:, :half], later], 1).reshape(total, part)
@@ -297,7 +326,7 @@
         (crossed, rotated, resid, lower_cols),
     )
     parts = over_mode(pieces)
-    gathered = over_cores(kernel(last, struct((modes + 1) * half, part), (crossed, parts)))
+    gathered = over_cores(kernel(last, struct((modes + 1) * few, part), (crossed, parts)))
     out, factor = kernel(
         functools.partial(finish, scale),
         (struct(width, rows), struct(count, count)),

time: 95.5 us -> 95.2 us (level)
  blocking collectives: 67.4 us -> 52.2 us
  waiting for transfers between devices: 8.14 us -> 16.6 us
  starting transfers between devices: 5.74 us -> 12.5 us
  local copies, waits for them, and re-layouts: 2.08 us -> 1.04 us
    all_to_all x2 -> x1, blocking collectives: 30.3 us -> 15.2 us  [over_mode(): return lax.all_to_all(block, MODE, 0, 0, tiled=True)]
    all_to_all x0 -> x1, waiting for transfers between devices: none -> 8.98 us  [over_mode(): return lax.all_to_all(block, MODE, 0, 0, tiled=True)]
    all_to_all x0 -> x1, starting transfers between devices: none -> 6.76 us  [over_mode(): return lax.all_to_all(block, MODE, 0, 0, tiled=True)]
    unnamed x2 -> x0, local copies, waits for them, and re-layouts: 1.04 us -> none
  transfers between devices with their start and end apart: 1 -> 2, of which waited for: 1 -> 2; matrix products, arithmetic and copies ran while one was open for 5% -> 5% of each run, Pallas kernels for 0% -> 0%
where the time goes in v6:
time: 95.2 us; the launch traced here: 94.4 us
  blocking collectives  52.2 us (55%)
  waiting for transfers between devices  16.6 us (17%)
  starting transfers between devices  12.5 us (13%)
  Pallas kernels  7.66 us (8%)
  matrix products  3.55 us (4%)
  local copies, waits for them, and re-layouts  1.04 us (1%)
    all_to_all x1, blocking collectives, cross(): lax.all_to_all(block, (Z, CORE) + MODE, 0, 0, tiled=True, axis_index_grou...  22.1 us
    all_to_all x1, blocking collectives, over_mode(): return lax.all_to_all(block, MODE, 0, 0, tiled=True)  15.2 us
    all_gather x4, blocking collectives, over_cores(): return lax.all_gather(block, CORE, axis=0, tiled=False)  14.9 us
    all_to_all x1, waiting for transfers between devices, over_mode(): return lax.all_to_all(block, MODE, 0, 0, tiled=True)  8.98 us
    pallas_call x9, Pallas kernels, kernel(): pl.pallas_call(body, out_shape=out, in_specs=specs or [VMEM] * len(args),...  7.66 us
    all_to_all x1, waiting for transfers between devices, cross(): lax.all_to_all(block, (Z, CORE) + MODE, 0, 0, tiled=True, axis_index_grou...  7.62 us
    all_to_all x1, starting transfers between devices, over_mode(): return lax.all_to_all(block, MODE, 0, 0, tiled=True)  6.76 us
    all_to_all x1, starting transfers between devices, cross(): lax.all_to_all(block, (Z, CORE) + MODE, 0, 0, tiled=True, axis_index_grou...  5.75 us
  transfers between devices with their start and end apart: 2, of which 2 were waited for; matrix products, arithmetic and copies ran while one was open for 5% of the time, Pallas kernels for 0%

profile of v6, /device:TPU:1, one launch (start us, length us, event | category | flops | bytes accessed | tf_op | source)
XLA Modules:
  0.0 94.4 jit_solution(14835750519439081708)
XLA Ops:
  0.6 1.9 %shard_map.50 = (f32[544,128]{1,0:T(8,128)S(1)}, f32[16,32,128]{2,1,0:T(8,128)S(1)}, f32[64,128]{1,0:T(8,128)S(1)}) custom-call(f32[64,2048]{1,0:T(8,128)} %bitcast.18, f32[64,2048]{1,0:T(8,128)} %bitcast.19), custom_call_target="tpu_custom_call" | custom-call | tf_op jit(solution)/shard_map/pallas_call | solution.py:251
  2.5 8.7 %all-gather = f32[1088,128]{1,0:T(8,128)S(1)} all-gather(f32[544,128]{1,0:T(8,128)S(1)} %get-tuple-element.11.first_ref), channel_id=2, replica_groups=mesh['z'=16,'core'=2,'y'=4,'x'=4] {'core'}, dimensions={0}, use_global_device_ids=true | all-gather | bytes 835584 | tf_op jit(solution)/shard_map/all_gather | solution.py:278
  11.2 22.1 %all_to_all.20.crossed_ref = f32[16,32,128]{2,1,0:T(8,128)S(1)} all-to-all(f32[16,32,128]{2,1,0:T(8,128)S(1)} %shard_map.51), channel_id=1, replica_groups={{16,48,80,112,144,176,208,240,272,304,336,368,400,432,464,496},{17,49,8..., dimensions={0} | all-to-all | bytes 524288 | tf_op jit(solution)/shard_map/all_to_all | solution.py:272
  33.4 0.9 shard_map.52
  34.2 6.8 %all-to-all-start.1 = ((f32[16,64,128]{2,1,0:T(8,128)}), f32[16,64,128]{2,1,0:T(8,128)S(1)}, u32[]{:S(2)}, u32[]{:S(2)}) async-start(f32[16,64,128]{2,1,0:T(8,128)} %shard_map.52), calls=%async_computation.1 | async-start | bytes 1048576 | tf_op jit(solution)/shard_map/all_to_all | solution.py:282
  41.0 9.0 %all-to-all-done.1.got_ref = f32[16,64,128]{2,1,0:T(8,128)S(1)} async-done(((f32[16,64,128]{2,1,0:T(8,128)}), f32[16,64,128]{2,1,0:T(8,128)S(1)}, u32[]{:S(2)}, u32[]{:S(2)}) %all-to-all-start.1) | async-done | bytes 524320 | tf_op jit(solution)/shard_map/all_to_all | solution.py:282
  50.0 2.2 %all-gather.1 = f32[32,32,128]{2,1,0:T(8,128)S(1)} all-gather(f32[16,32,128]{2,1,0:T(8,128)S(1)} %shard_map.53), channel_id=3, replica_groups=mesh['z'=16,'core'=2,'y'=4,'x'=4] {'core'}, dimensions={0}, use_global_device_ids=true | all-gather | bytes 786432 | tf_op jit(solution)/shard_map/all_gather | solution.py:278
  52.2 0.6 shard_map.54
  52.8 1.9 %all-gather.2 = f32[96,128]{1,0:T(8,128)S(1)} all-gather(f32[48,128]{1,0:T(8,128)S(1)} %get-tuple-element.14), channel_id=4, replica_groups=mesh['z'=16,'core'=2,'y'=4,'x'=4] {'core'}, dimensions={0}, use_global_device_ids=true | all-gather | bytes 73728 | tf_op jit(solution)/shard_map/all_gather | solution.py:278
  54.6 0.7 shard_map.55
  55.3 5.7 %all-to-all-start.2 = ((f32[16,24,128]{2,1,0:T(8,128)}), f32[16,24,128]{2,1,0:T(8,128)S(1)}, u32[]{:S(2)}, u32[]{:S(2)}) async-start(f32[16,24,128]{2,1,0:T(8,128)} %shard_map.55), calls=%async_computation.2 | async-start | bytes 393216 | tf_op jit(solution)/shard_map/all_to_all | solution.py:272
  61.1 0.8 constant_dynamic-slice_fusion.cols_ref
  61.9 0.1 fusion.5
  62.0 3.6 %fusion.2 = f32[1024,128]{0,1:T(8,128)S(1)} fusion(f32[1024,128]{1,0:T(8,128)S(1)} %bitcast.17, f32[1088,1024]{1,0:T(8,128)} %param.5), kind=kOutput, calls=%fused_computation.2 | convolution fusion | flops 805306368 | bytes 5242880 | tf_op jit(solution)/shard_map/dot_general | solution.py:28
  65.6 0.2 copy.6
  65.8 7.6 %all-to-all-done.2.crossed_ref = f32[16,24,128]{2,1,0:T(8,128)S(1)} async-done(((f32[16,24,128]{2,1,0:T(8,128)}), f32[16,24,128]{2,1,0:T(8,128)S(1)}, u32[]{:S(2)}, u32[]{:S(2)}) %all-to-all-start.2) | async-done | bytes 196640 | tf_op jit(solution)/shard_map/all_to_all | solution.py:272
  73.4 0.1 shard_map.56
  73.5 15.2 %all_to_all.21.parts_ref = f32[16,128,128]{2,1,0:T(8,128)S(1)} all-to-all(f32[16,128,128]{2,1,0:T(8,128)S(1)} %get-tuple-element.16), channel_id=1, replica_groups=mesh['z'=16,'core'=2,'y'=4,'x'=4] {'y','x'}, dimensions={0} | all-to-all | bytes 2097152 | tf_op jit(solution)/shard_map/all_to_all | solution.py:282
  88.8 2.1 %all-gather.3 = f32[816,128]{1,0:T(8,128)S(1)} all-gather(f32[408,128]{1,0:T(8,128)S(1)} %shard_map.57), channel_id=5, replica_groups=mesh['z'=16,'core'=2,'y'=4,'x'=4] {'core'}, dimensions={0}, use_global_device_ids=true | all-gather | bytes 626688 | tf_op jit(solution)/shard_map/all_gather | solution.py:278
  90.9 3.5 %shard_map.58 = (f32[64,2048]{1,0:T(8,128)}, f32[64,64]{1,0:T(8,128)}) custom-call(f32[2,408,128]{2,1,0:T(8,128)S(1)} %bitcast.15, f32[64,64]{1,0:T(8,128)S(1)} %get-tuple-element.17.lower_cols_ref, f32[16,128,128]{2,1,0:T(8,128)S(1)} %all_to_all.21.parts_ref), custom_call_target="tpu_custom_call" | custom-call | tf_op jit(solution)/shard_map/pallas_call | solution.py:251
  (4 shorter events, 0.1 us)
Async XLA Ops:
  34.2 15.8 %all-to-all-start.1 = ((f32[16,64,128]{2,1,0:T(8,128)}), f32[16,64,128]{2,1,0:T(8,128)S(1)}, u32[]{:S(2)}, u32[]{:S(2)}) async-start(f32[16,64,128]{2,1,0:T(8,128)} %shard_map.52), calls=%async_computation.1 | async-start | bytes 1048576 | tf_op jit(solution)/shard_map/all_to_all | solution.py:282
  55.3 18.1 %all-to-all-start.2 = ((f32[16,24,128]{2,1,0:T(8,128)}), f32[16,24,128]{2,1,0:T(8,128)S(1)}, u32[]{:S(2)}, u32[]{:S(2)}) async-start(f32[16,24,128]{2,1,0:T(8,128)} %shard_map.55), calls=%async_computation.2 | async-start | bytes 393216 | tf_op jit(solution)/shard_map/all_to_all | solution.py:272

commit v7 on v6

--- a/solution.py
+++ b/solution.py
@@ -74,7 +74,9 @@
     )
 
 
-def project(bt_ref, st_ref, first_ref, early_ref, own_ref, b_buf, s_buf, sems):
+def project(
+    bt_ref, st_ref, rot_ref, first_ref, early_ref, own_ref, cols_ref, b_buf, s_buf, r_buf, sems
+):
     step = b_buf.shape[1] // CHUNKS
     copies = []
     for i in range(CHUNKS):
@@ -85,6 +87,14 @@
             copies.append(copy)
     _, half, part = early_ref.shape
     each = step // part
+    place = lax.axis_index("y") * lax.axis_size("x") + lax.axis_index("x")
+    count, width = cols_ref.shape
+    wide = r_buf.shape[1]
+    side = pl.ds(pl.multiple_of(place // (wide // width) * wide, wide), wide)
+    columns = pltpu.make_async_copy(
+        rot_ref.at[pl.ds(rot_ref.shape[0] - count, count), side], r_buf, sems.at[2 * CHUNKS]
+    )
+    columns.start()
     total = None
     for i in range(CHUNKS):
         copies[2 * i].wait()
@@ -98,8 +108,10 @@
             early_ref[j] = piece[:half]
             first_ref[(j + 1) * half : (j + 2) * half] = piece[half:]
     first_ref[:half] = pack(total)
-    place = lax.axis_index("y") * lax.axis_size("x") + lax.axis_index("x")
     own_ref[...] = s_buf[:, pl.ds(pl.multiple_of(place * part, part), part)]
+    columns.wait()
+    found = r_buf[...]
+    cols_ref[...] = jnp.where(place % 2 == 0, found[:, :width], found[:, width:])
 
 
 def first_core():
@@ -159,7 +171,7 @@
     both_ref[few:] = resid[count - few :]
 
 
-def bundle_back(crossed_ref, rotated_ref, resid_ref, cols_ref, out_ref, cols_out_ref):
+def bundle_back(crossed_ref, rotated_ref, resid_ref, out_ref):
     width, few = rotated_ref.shape[1], crossed_ref.shape[1]
     gram = added(crossed_ref)
     out_ref[:, :width] = rotated_ref[...]
@@ -169,7 +181,6 @@
     for j in range(out_ref.shape[0]):
         out_ref[j, width : width + cut] = early
         out_ref[j, width + cut :] = late
-    cols_out_ref[...] = cols_ref[...]
 
 
 def last(crossed_ref, parts_ref, out_ref):
@@ -291,19 +302,24 @@
     half = width // 2
     few = 3 * count // 8
     total = rotation.shape[1]
-    place = lax.axis_index(MODE)
     scale = float(rows * depth * 2) ** 0.5
     bt, st = basis.T, snapshots.T
     buffers = (
         pltpu.VMEM((width, rows), jnp.float32),
         pltpu.VMEM((count, rows), jnp.float32),
-        pltpu.SemaphoreType.DMA((2 * CHUNKS,)),
-    )
-    first, early, st_own = kernel(
+        pltpu.VMEM((count, 2 * width), jnp.float32),
+        pltpu.SemaphoreType.DMA((2 * CHUNKS + 1,)),
+    )
+    first, early, st_own, lower_cols = kernel(
         project,
-        (struct((modes + 1) * half, part), struct(modes, half, part), struct(count, part)),
-        (bt, st),
-        [HBM, HBM],
+        (
+            struct((modes + 1) * half, part),
+            struct(modes, half, part),
+            struct(count, part),
+            struct(count, width),
+        ),
+        (bt, st, rotation),
+        [HBM] * 3,
         buffers,
         FULL,
     )
@@ -319,11 +335,8 @@
     later = jnp.where(lax.axis_index(CORE) == 0, got[:, half:], traded[0])
     own = jnp.concatenate([got[:, :half], later], 1).reshape(total, part)
     rotated = dot(rotation[:total], own, 0, 0).reshape(modes, width, part)
-    lower_cols = lax.dynamic_slice(rotation, (total, place * width), (count, width))
-    pieces, lower_cols = kernel(
-        bundle_back,
-        (struct(modes, width + count, part), struct(count, width)),
-        (crossed, rotated, resid, lower_cols),
+    pieces = kernel(
+        bundle_back, struct(modes, width + count, part), (crossed, rotated, resid)
     )
     parts = over_mode(pieces)
     gathered = over_cores(kernel(last, struct((modes + 1) * few, part), (crossed, parts)))

time: 95.2 us -> 93.8 us (0.985)
  blocking collectives: 52.2 us -> 67.2 us
  waiting for transfers between devices: 16.6 us -> 8.54 us
  starting transfers between devices: 12.5 us -> 6.04 us
    all_to_all x1 -> x2, blocking collectives: 15.2 us -> 30.2 us  [over_mode(): return lax.all_to_all(block, MODE, 0, 0, tiled=True)]
    all_to_all x1 -> x0, waiting for transfers between devices: 8.98 us -> none  [over_mode(): return lax.all_to_all(block, MODE, 0, 0, tiled=True)]
    all_to_all x1 -> x0, starting transfers between devices: 6.76 us -> none  [over_mode(): return lax.all_to_all(block, MODE, 0, 0, tiled=True)]
  transfers between devices with their start and end apart: 2 -> 1, of which waited for: 2 -> 1; matrix products, arithmetic and copies ran while one was open for 5% -> 4% of each run, Pallas kernels for 0% -> 0%
where the time goes in v7:
time: 93.8 us; the launch traced here: 93.2 us
  blocking collectives  67.2 us (72%)
  waiting for transfers between devices  8.54 us (9%)
  Pallas kernels  6.95 us (7%)
  starting transfers between devices  6.04 us (6%)
  matrix products  3.47 us (4%)
    all_to_all x2, blocking collectives, over_mode(): return lax.all_to_all(block, MODE, 0, 0, tiled=True)  30.2 us
    all_to_all x1, blocking collectives, cross(): lax.all_to_all(block, (Z, CORE) + MODE, 0, 0, tiled=True, axis_index_grou...  22.1 us
    all_gather x4, blocking collectives, over_cores(): return lax.all_gather(block, CORE, axis=0, tiled=False)  14.9 us
    all_to_all x1, waiting for transfers between devices, cross(): lax.all_to_all(block, (Z, CORE) + MODE, 0, 0, tiled=True, axis_index_grou...  8.54 us
    pallas_call x9, Pallas kernels, kernel(): pl.pallas_call(body, out_shape=out, in_specs=specs or [VMEM] * len(args),...  6.95 us
    all_to_all x1, starting transfers between devices, cross(): lax.all_to_all(block, (Z, CORE) + MODE, 0, 0, tiled=True, axis_index_grou...  6.04 us
    dot_general x1, matrix products, dot(): lax.dot_general(a, b, (((left,), (right,)), ((), ())), precision=HIGH)  3.47 us
  transfers between devices with their start and end apart: 1, of which 1 were waited for; matrix products, arithmetic and copies ran while one was open for 4% of the time, Pallas kernels for 0%

profile of v7, /device:TPU:1, one launch (start us, length us, event | category | flops | bytes accessed | tf_op | source)
XLA Modules:
  0.0 93.2 jit_solution(13191567461668530865)
XLA Ops:
  0.6 1.9 %shard_map.50 = (f32[544,128]{1,0:T(8,128)S(1)}, f32[16,32,128]{2,1,0:T(8,128)S(1)}, f32[64,128]{1,0:T(8,128)S(1)}, f32[64,64]{1,0:T(8,128)S(1)}) custom-call(f32[64,2048]{1,0:T(8,128)} %bitcast.18, f32[64,2048]{1,0:T(8,128)} %bitcast.19, f32[1088,1024]{1,0:T(8,128)} %rot_ref.1), custom_call_target="tpu_custom_call" | custom-call | tf_op jit(solution)/shard_map/pallas_call | solution.py:262
  2.6 8.7 %all-gather = f32[1088,128]{1,0:T(8,128)S(1)} all-gather(f32[544,128]{1,0:T(8,128)S(1)} %get-tuple-element.10.first_ref), channel_id=2, replica_groups=mesh['z'=16,'core'=2,'y'=4,'x'=4] {'core'}, dimensions={0}, use_global_device_ids=true | all-gather | bytes 835584 | tf_op jit(solution)/shard_map/all_gather | solution.py:289
  11.3 22.1 %all_to_all.20.crossed_ref = f32[16,32,128]{2,1,0:T(8,128)S(1)} all-to-all(f32[16,32,128]{2,1,0:T(8,128)S(1)} %shard_map.51), channel_id=1, replica_groups={{16,48,80,112,144,176,208,240,272,304,336,368,400,432,464,496},{17,49,8..., dimensions={0} | all-to-all | bytes 524288 | tf_op jit(solution)/shard_map/all_to_all | solution.py:283
  33.4 0.1 shard_map.52
  33.5 15.5 %all_to_all.21.got_ref = f32[16,64,128]{2,1,0:T(8,128)S(1)} all-to-all(f32[16,64,128]{2,1,0:T(8,128)S(1)} %shard_map.52), channel_id=1, replica_groups=mesh['z'=16,'core'=2,'y'=4,'x'=4] {'y','x'}, dimensions={0} | all-to-all | bytes 1048576 | tf_op jit(solution)/shard_map/all_to_all | solution.py:293
  49.1 2.2 %all-gather.1 = f32[32,32,128]{2,1,0:T(8,128)S(1)} all-gather(f32[16,32,128]{2,1,0:T(8,128)S(1)} %shard_map.53), channel_id=3, replica_groups=mesh['z'=16,'core'=2,'y'=4,'x'=4] {'core'}, dimensions={0}, use_global_device_ids=true | all-gather | bytes 786432 | tf_op jit(solution)/shard_map/all_gather | solution.py:289
  51.3 0.6 shard_map.54
  51.8 1.9 %all-gather.2 = f32[96,128]{1,0:T(8,128)S(1)} all-gather(f32[48,128]{1,0:T(8,128)S(1)} %get-tuple-element.13), channel_id=4, replica_groups=mesh['z'=16,'core'=2,'y'=4,'x'=4] {'core'}, dimensions={0}, use_global_device_ids=true | all-gather | bytes 73728 | tf_op jit(solution)/shard_map/all_gather | solution.py:289
  53.7 0.7 shard_map.55
  54.4 6.0 %all-to-all-start.2 = ((f32[16,24,128]{2,1,0:T(8,128)}), f32[16,24,128]{2,1,0:T(8,128)S(1)}, u32[]{:S(2)}, u32[]{:S(2)}) async-start(f32[16,24,128]{2,1,0:T(8,128)} %shard_map.55), calls=%async_computation.2 | async-start | bytes 393216 | tf_op jit(solution)/shard_map/all_to_all | solution.py:283
  60.5 0.1 fusion.5
  60.6 3.5 %fusion.2 = f32[1024,128]{0,1:T(8,128)S(1)} fusion(f32[1024,128]{1,0:T(8,128)S(1)} %bitcast.17, f32[1088,1024]{1,0:T(8,128)} %rot_ref.1), kind=kOutput, calls=%fused_computation.2 | convolution fusion | flops 805306368 | bytes 5242880 | tf_op jit(solution)/shard_map/dot_general | solution.py:28
  64.1 0.2 copy.6
  64.3 8.5 %all-to-all-done.2.crossed_ref = f32[16,24,128]{2,1,0:T(8,128)S(1)} async-done(((f32[16,24,128]{2,1,0:T(8,128)}), f32[16,24,128]{2,1,0:T(8,128)S(1)}, u32[]{:S(2)}, u32[]{:S(2)}) %all-to-all-start.2) | async-done | bytes 196640 | tf_op jit(solution)/shard_map/all_to_all | solution.py:283
  72.8 0.1 shard_map.56
  72.9 14.6 %all_to_all.22.parts_ref = f32[16,128,128]{2,1,0:T(8,128)S(1)} all-to-all(f32[16,128,128]{2,1,0:T(8,128)S(1)} %shard_map.56), channel_id=1, replica_groups=mesh['z'=16,'core'=2,'y'=4,'x'=4] {'y','x'}, dimensions={0} | all-to-all | bytes 2097152 | tf_op jit(solution)/shard_map/all_to_all | solution.py:293
  87.6 2.1 %all-gather.3 = f32[816,128]{1,0:T(8,128)S(1)} all-gather(f32[408,128]{1,0:T(8,128)S(1)} %shard_map.57), channel_id=5, replica_groups=mesh['z'=16,'core'=2,'y'=4,'x'=4] {'core'}, dimensions={0}, use_global_device_ids=true | all-gather | bytes 626688 | tf_op jit(solution)/shard_map/all_gather | solution.py:289
  89.7 3.5 %shard_map.58 = (f32[64,2048]{1,0:T(8,128)}, f32[64,64]{1,0:T(8,128)}) custom-call(f32[2,408,128]{2,1,0:T(8,128)S(1)} %bitcast.15, f32[64,64]{1,0:T(8,128)S(1)} %get-tuple-element.15.lower_cols_ref, f32[16,128,128]{2,1,0:T(8,128)S(1)} %all_to_all.22.parts_ref), custom_call_target="tpu_custom_call" | custom-call | tf_op jit(solution)/shard_map/pallas_call | solution.py:262
  (4 shorter events, 0.1 us)
Async XLA Ops:
  54.4 18.4 %all-to-all-start.2 = ((f32[16,24,128]{2,1,0:T(8,128)}), f32[16,24,128]{2,1,0:T(8,128)S(1)}, u32[]{:S(2)}, u32[]{:S(2)}) async-start(f32[16,24,128]{2,1,0:T(8,128)} %shard_map.55), calls=%async_computation.2 | async-start | bytes 393216 | tf_op jit(solution)/shard_map/all_to_all | solution.py:283

commit v8 on v7

--- a/solution.py
+++ b/solution.py
@@ -48,29 +48,40 @@
     return jnp.concatenate([block[:half], block[half:]], 1)
 
 
+def square(size):
+    return [lax.broadcasted_iota(jnp.int32, (size, size), d) for d in range(2)]
+
+
 def pack_symmetric(block):
     half = block.shape[0] // 2
-    cut = 3 * half // 4
-    quarters = (block[:half, :half], block[half:, :half], block[half:, half:])
-    side = jnp.concatenate([quarter[cut:] for quarter in quarters], 0)
-    return jnp.concatenate([quarter[:cut] for quarter in quarters] + [side], 1)
+    step = half // 2
+    row, col = square(half)
+    last_quarter = block[half:, half:]
+    mixed = jnp.where(row >= col, block[:half, :half], last_quarter)
+    cross = block[half:, :half]
+    diagonal = jnp.sum(jnp.where(row == col, last_quarter, 0.0), 0, keepdims=True)
+    top = [mixed[:step], mixed[step:], cross[:step], cross[step:]]
+    rest = [jnp.broadcast_to(diagonal, (8, half)), jnp.zeros((8, 3 * half), jnp.float32)]
+    return jnp.concatenate([jnp.concatenate(top, 1), jnp.concatenate(rest, 1)], 0)
 
 
 def unpack_symmetric(packed):
     half = packed.shape[1] // 4
-    step = packed.shape[0] // 3
-    first, cross, second = (
+    step = half // 2
+    row, col = square(half)
+    mixed, cross = (
         jnp.concatenate(
-            [
-                packed[:, k * half : (k + 1) * half],
-                packed[k * step : (k + 1) * step, 3 * half :],
-            ],
-            0,
+            [packed[:step, k * half : (k + 1) * half] for k in (first, first + 1)], 0
         )
-        for k in range(3)
-    )
+        for first in (0, 2)
+    )
+    turned = mixed.T
+    first = jnp.where(row >= col, mixed, turned)
+    last_quarter = jnp.where(row < col, mixed, turned)
+    diagonal = jnp.broadcast_to(packed[step : step + 1, :half], (half, half))
+    last_quarter = jnp.where(row == col, diagonal, last_quarter)
     return jnp.concatenate(
-        [jnp.concatenate([first, cross.T], 1), jnp.concatenate([cross, second], 1)], 0
+        [jnp.concatenate([first, cross.T], 1), jnp.concatenate([cross, last_quarter], 1)], 0
     )
 
 
@@ -126,18 +137,38 @@
         out_ref[k] = jnp.where(first_core(), piece, coeffs)
 
 
+def flat(block, first, used):
+    return jnp.concatenate([block[r : r + 1] for r in range(first, first + used)], 1)
+
+
+def stacked(row, part, above, below):
+    pieces = [row[:, r : r + part] for r in range(0, row.shape[1], part)]
+    if above:
+        pieces = [jnp.zeros((above, part), jnp.float32)] + pieces
+    if below:
+        pieces = pieces + [jnp.zeros((below, part), jnp.float32)]
+    return jnp.concatenate(pieces, 0)
+
+
+def patched(block, spare, rows):
+    place = lax.broadcasted_iota(jnp.int32, block.shape, 0)
+    return jnp.where(first_core(), block, jnp.where(place < spare, block, rows))
+
+
 def share_back(both_ref, out_ref):
-    few = out_ref.shape[1]
+    few = both_ref.shape[1] // 2
+    used = out_ref.shape[2] // both_ref.shape[2]
     gram = both_ref[0, :few] + both_ref[1, :few]
-    mine = jnp.where(first_core(), both_ref[1, few:], gram)
+    late = both_ref[1, few:]
+    row = jnp.where(first_core(), flat(late, few - used, used), flat(gram, 0, used))
     for k in range(out_ref.shape[0]):
-        out_ref[k] = mine
-
-
-def added(ref):
-    total = ref[0]
+        out_ref[k] = row
+
+
+def added(ref, start=0):
+    total = ref[0, start:]
     for k in range(1, ref.shape[0]):
-        total = total + ref[k]
+        total = total + ref[k, start:]
     return total
 
 
@@ -153,6 +184,13 @@
 def trade(crossed_ref, got_ref, out_ref):
     half = crossed_ref.shape[1]
     out_ref[...] = jnp.where(first_core(), crossed_ref[...], got_ref[:, half:])
+
+
+def join(got_ref, traded_ref, out_ref):
+    half = traded_ref.shape[2]
+    late = jnp.where(first_core(), got_ref[:, half:], traded_ref[0])
+    rows = jnp.concatenate([got_ref[:, :half], late], 1)
+    out_ref[...] = rows.reshape(out_ref.shape)
 
 
 def remainder(got_ref, traded_ref, st_ref, resid_ref, both_ref):
@@ -172,25 +210,26 @@
 
 
 def bundle_back(crossed_ref, rotated_ref, resid_ref, out_ref):
-    width, few = rotated_ref.shape[1], crossed_ref.shape[1]
-    gram = added(crossed_ref)
+    modes, width, part = rotated_ref.shape
+    count = resid_ref.shape[0]
+    used = crossed_ref.shape[2] // part
+    few = (used + 7) // 8 * 8
+    gram = stacked(added(crossed_ref), part, few - used, 0)
+    early = resid_ref[: count - few]
+    late = patched(resid_ref[count - few :], few - used, gram)
     out_ref[:, :width] = rotated_ref[...]
-    cut = resid_ref.shape[0] - few
-    early = resid_ref[:cut]
-    late = jnp.where(first_core(), resid_ref[cut:], gram)
-    for j in range(out_ref.shape[0]):
-        out_ref[j, width : width + cut] = early
-        out_ref[j, width + cut :] = late
+    for j in range(modes):
+        out_ref[j, width : width + count - few] = early
+        out_ref[j, width + count - few :] = late
 
 
 def last(crossed_ref, parts_ref, out_ref):
-    modes, few, part = crossed_ref.shape
-    out_ref[: modes * few] = crossed_ref[...].reshape(modes * few, part)
-    start = parts_ref.shape[1] - few
-    total = parts_ref[0, start:]
-    for j in range(1, modes):
-        total = total + parts_ref[j, start:]
-    out_ref[modes * few :] = total
+    modes = crossed_ref.shape[0]
+    used = crossed_ref.shape[2] // parts_ref.shape[2]
+    few = (used + 7) // 8 * 8
+    out_ref[:modes] = crossed_ref[...]
+    gram = added(parts_ref, parts_ref.shape[1] - few)
+    out_ref[modes] = flat(gram, few - used, used)
 
 
 def eliminate(gram):
@@ -245,15 +284,16 @@
 def finish(scale, last_ref, lower_cols_ref, parts_ref, out_ref, factor_ref):
     count, width = lower_cols_ref.shape
     modes, _, part = parts_ref.shape
-    few = last_ref.shape[1] // (modes + 1)
+    used = last_ref.shape[3] // part
+    few = (used + 7) // 8 * 8
     cut = width + count - few
-    done = eliminate(unpack_symmetric(last_ref[1, modes * few :]))
+    gram = stacked(last_ref[1, modes], part, 0, few - used)
+    done = eliminate(unpack_symmetric(gram))
     factor_ref[...] = done[:, :count].T * (1.0 / scale)
     weights = dot3(lower_cols_ref[...].T, done[:, count:]) * scale
     for j in range(modes):
-        late = jnp.where(
-            first_core(), parts_ref[j, cut:], last_ref[0, j * few : (j + 1) * few]
-        )
+        late = stacked(last_ref[0, j], part, few - used, 0)
+        late = patched(parts_ref[j, cut:], few - used, late)
         resid = jnp.concatenate([parts_ref[j, width:cut], late], 0)
         out_ref[:, j * part : (j + 1) * part] = parts_ref[j, :width] * scale + dot3(weights, resid)
 
@@ -301,6 +341,7 @@
     part = rows // modes
     half = width // 2
     few = 3 * count // 8
+    used = count // 4 + 1
     total = rotation.shape[1]
     scale = float(rows * depth * 2) ** 0.5
     bt, st = basis.T, snapshots.T
@@ -330,16 +371,15 @@
     resid, both = kernel(
         remainder, (struct(count, part), struct(2 * few, part)), (got, traded, st_own)
     )
-    crossed = kernel(share_back, struct(depth, few, part), (over_cores(both),))
+    crossed = kernel(share_back, struct(depth, 1, used * part), (over_cores(both),))
     crossed = cross(crossed, depth, modes)
-    later = jnp.where(lax.axis_index(CORE) == 0, got[:, half:], traded[0])
-    own = jnp.concatenate([got[:, :half], later], 1).reshape(total, part)
+    own = kernel(join, struct(total, part), (got, traded))
     rotated = dot(rotation[:total], own, 0, 0).reshape(modes, width, part)
     pieces = kernel(
         bundle_back, struct(modes, width + count, part), (crossed, rotated, resid)
     )
     parts = over_mode(pieces)
-    gathered = over_cores(kernel(last, struct((modes + 1) * few, part), (crossed, parts)))
+    gathered = over_cores(kernel(last, struct(modes + 1, 1, used * part), (crossed, parts)))
     out, factor = kernel(
         functools.partial(finish, scale),
         (struct(width, rows), struct(count, count)),

time: 93.8 us -> 93.5 us (level)
    pallas_call x9 -> x10, Pallas kernels: 6.95 us -> 7.09 us  [kernel(): pl.pallas_call(body, out_shape=out, in_specs=specs or [VMEM] * len(args),...]
where the time goes in v8:
time: 93.5 us; the launch traced here: 92.9 us
  blocking collectives  67.1 us (72%)
  waiting for transfers between devices  8.28 us (9%)
  Pallas kernels  7.09 us (8%)
  starting transfers between devices  6.04 us (6%)
  matrix products  3.47 us (4%)
    all_to_all x2, blocking collectives, over_mode(): return lax.all_to_all(block, MODE, 0, 0, tiled=True)  30.3 us
    all_to_all x1, blocking collectives, cross(): lax.all_to_all(block, (Z, CORE) + MODE, 0, 0, tiled=True, axis_index_grou...  22.1 us
    all_gather x4, blocking collectives, over_cores(): return lax.all_gather(block, CORE, axis=0, tiled=False)  14.7 us
    all_to_all x1, waiting for transfers between devices, cross(): lax.all_to_all(block, (Z, CORE) + MODE, 0, 0, tiled=True, axis_index_grou...  8.28 us
    pallas_call x10, Pallas kernels, kernel(): pl.pallas_call(body, out_shape=out, in_specs=specs or [VMEM] * len(args),...  7.09 us
    all_to_all x1, starting transfers between devices, cross(): lax.all_to_all(block, (Z, CORE) + MODE, 0, 0, tiled=True, axis_index_grou...  6.04 us
    dot_general x1, matrix products, dot(): lax.dot_general(a, b, (((left,), (right,)), ((), ())), precision=HIGH)  3.47 us
  transfers between devices with their start and end apart: 1, of which 1 were waited for; matrix products, arithmetic and copies ran while one was open for 4% of the time, Pallas kernels for 0%

profile of v8, /device:TPU:1, one launch (start us, length us, event | category | flops | bytes accessed | tf_op | source)
XLA Modules:
  0.0 92.9 jit_solution(15709651661715067447)
XLA Ops:
  0.6 1.9 %shard_map.50 = (f32[544,128]{1,0:T(8,128)S(1)}, f32[16,32,128]{2,1,0:T(8,128)S(1)}, f32[64,128]{1,0:T(8,128)S(1)}, f32[64,64]{1,0:T(8,128)S(1)}) custom-call(f32[64,2048]{1,0:T(8,128)} %bitcast.17, f32[64,2048]{1,0:T(8,128)} %bitcast.18, f32[1088,1024]{1,0:T(8,128)} %rot_ref.1), custom_call_target="tpu_custom_call" | custom-call | tf_op jit(solution)/shard_map/pallas_call | solution.py:302
  2.6 8.7 %all-gather = f32[1088,128]{1,0:T(8,128)S(1)} all-gather(f32[544,128]{1,0:T(8,128)S(1)} %get-tuple-element.10.first_ref), channel_id=2, replica_groups=mesh['z'=16,'core'=2,'y'=4,'x'=4] {'core'}, dimensions={0}, use_global_device_ids=true | all-gather | bytes 835584 | tf_op jit(solution)/shard_map/all_gather | solution.py:329
  11.3 22.1 %all_to_all.20.crossed_ref = f32[16,32,128]{2,1,0:T(8,128)S(1)} all-to-all(f32[16,32,128]{2,1,0:T(8,128)S(1)} %shard_map.51), channel_id=1, replica_groups={{16,48,80,112,144,176,208,240,272,304,336,368,400,432,464,496},{17,49,8..., dimensions={0} | all-to-all | bytes 524288 | tf_op jit(solution)/shard_map/all_to_all | solution.py:323
  33.4 0.1 shard_map.52
  33.5 15.5 %all_to_all.21.got_ref = f32[16,64,128]{2,1,0:T(8,128)S(1)} all-to-all(f32[16,64,128]{2,1,0:T(8,128)S(1)} %shard_map.52), channel_id=1, replica_groups=mesh['z'=16,'core'=2,'y'=4,'x'=4] {'y','x'}, dimensions={0} | all-to-all | bytes 1048576 | tf_op jit(solution)/shard_map/all_to_all | solution.py:333
  49.1 2.2 %all-gather.1 = f32[32,32,128]{2,1,0:T(8,128)S(1)} all-gather(f32[16,32,128]{2,1,0:T(8,128)S(1)} %shard_map.53), channel_id=3, replica_groups=mesh['z'=16,'core'=2,'y'=4,'x'=4] {'core'}, dimensions={0}, use_global_device_ids=true | all-gather | bytes 786432 | tf_op jit(solution)/shard_map/all_gather | solution.py:329
  51.3 0.6 shard_map.54
  51.9 1.8 %all-gather.2 = f32[96,128]{1,0:T(8,128)S(1)} all-gather(f32[48,128]{1,0:T(8,128)S(1)} %get-tuple-element.13), channel_id=4, replica_groups=mesh['z'=16,'core'=2,'y'=4,'x'=4] {'core'}, dimensions={0}, use_global_device_ids=true | all-gather | bytes 73728 | tf_op jit(solution)/shard_map/all_gather | solution.py:329
  53.7 0.7 shard_map.55
  54.4 6.0 %all-to-all-start.2 = ((f32[16,1,2176]{2,1,0:T(1,128)}), f32[16,1,2176]{2,1,0:T(1,128)S(1)}, u32[]{:S(2)}, u32[]{:S(2)}) async-start(f32[16,1,2176]{2,1,0:T(1,128)} %shard_map.55), calls=%async_computation.2 | async-start | bytes 278528 | tf_op jit(solution)/shard_map/all_to_all | solution.py:323
  60.5 3.5 %fusion.2 = f32[1024,128]{0,1:T(8,128)S(1)} fusion(f32[1024,128]{1,0:T(8,128)S(1)} %shard_map.56, f32[1088,1024]{1,0:T(8,128)} %rot_ref.1), kind=kOutput, calls=%fused_computation.2 | convolution fusion | flops 805306368 | bytes 5242880 | tf_op jit(solution)/shard_map/dot_general | solution.py:28
  64.0 0.2 copy.6
  64.2 8.3 %all-to-all-done.2.crossed_ref = f32[16,1,2176]{2,1,0:T(1,128)S(1)} async-done(((f32[16,1,2176]{2,1,0:T(1,128)}), f32[16,1,2176]{2,1,0:T(1,128)S(1)}, u32[]{:S(2)}, u32[]{:S(2)}) %all-to-all-start.2) | async-done | bytes 139296 | tf_op jit(solution)/shard_map/all_to_all | solution.py:323
  72.5 0.1 shard_map.57
  72.6 14.7 %all_to_all.22.parts_ref = f32[16,128,128]{2,1,0:T(8,128)S(1)} all-to-all(f32[16,128,128]{2,1,0:T(8,128)S(1)} %shard_map.57), channel_id=1, replica_groups=mesh['z'=16,'core'=2,'y'=4,'x'=4] {'y','x'}, dimensions={0} | all-to-all | bytes 2097152 | tf_op jit(solution)/shard_map/all_to_all | solution.py:333
  87.3 2.0 %all-gather.3 = f32[34,1,2176]{2,1,0:T(1,128)S(1)} all-gather(f32[17,1,2176]{2,1,0:T(1,128)S(1)} %shard_map.58), channel_id=5, replica_groups=mesh['z'=16,'core'=2,'y'=4,'x'=4] {'core'}, dimensions={0}, use_global_device_ids=true | all-gather | bytes 443904 | tf_op jit(solution)/shard_map/all_gather | solution.py:329
  89.3 3.5 %shard_map.59 = (f32[64,2048]{1,0:T(8,128)}, f32[64,64]{1,0:T(8,128)}) custom-call(f32[2,17,1,2176]{3,2,1,0:T(1,128)S(1)} %bitcast.15, f32[64,64]{1,0:T(8,128)S(1)} %get-tuple-element.15.lower_cols_ref, f32[16,128,128]{2,1,0:T(8,128)S(1)} %all_to_all.22.parts_ref), custom_call_target="tpu_custom_call" | custom-call | tf_op jit(solution)/shard_map/pallas_call | solution.py:302
  (4 shorter events, 0.2 us)
Async XLA Ops:
  54.4 18.1 %all-to-all-start.2 = ((f32[16,1,2176]{2,1,0:T(1,128)}), f32[16,1,2176]{2,1,0:T(1,128)S(1)}, u32[]{:S(2)}, u32[]{:S(2)}) async-start(f32[16,1,2176]{2,1,0:T(1,128)} %shard_map.55), calls=%async_computation.2 | async-start | bytes 278528 | tf_op jit(solution)/shard_map/all_to_all | solution.py:323

commit v9 on v8

--- a/solution.py
+++ b/solution.py
@@ -133,7 +133,7 @@
     count, half, _ = out_ref.shape
     coeffs = both_ref[0, :half] + both_ref[1, :half]
     for k in range(count):
-        piece = both_ref[1, (k + 1) * half : (k + 2) * half]
+        piece = both_ref[0, (k + 1) * half : (k + 2) * half]
         out_ref[k] = jnp.where(first_core(), piece, coeffs)
 
 
@@ -172,33 +172,28 @@
     return total
 
 
-def bundle(crossed_ref, first_ref, early_ref, out_ref):
+def bundle(crossed_ref, both_ref, early_ref, out_ref):
     half = crossed_ref.shape[1]
     coeffs = added(crossed_ref)
     out_ref[:, :half] = early_ref[...]
     for j in range(out_ref.shape[0]):
-        piece = first_ref[(j + 1) * half : (j + 2) * half]
+        piece = both_ref[1, (j + 1) * half : (j + 2) * half]
         out_ref[j, half:] = jnp.where(first_core(), piece, coeffs)
 
 
-def trade(crossed_ref, got_ref, out_ref):
-    half = crossed_ref.shape[1]
-    out_ref[...] = jnp.where(first_core(), crossed_ref[...], got_ref[:, half:])
-
-
-def join(got_ref, traded_ref, out_ref):
+def join(got_ref, crossed_ref, traded_ref, out_ref):
     half = traded_ref.shape[2]
-    late = jnp.where(first_core(), got_ref[:, half:], traded_ref[0])
+    late = jnp.where(first_core(), crossed_ref[...], traded_ref[0])
     rows = jnp.concatenate([got_ref[:, :half], late], 1)
     out_ref[...] = rows.reshape(out_ref.shape)
 
 
-def remainder(got_ref, traded_ref, st_ref, resid_ref, both_ref):
+def remainder(got_ref, crossed_ref, traded_ref, st_ref, resid_ref, both_ref):
     modes, width, part = got_ref.shape
     count = st_ref.shape[0]
     half = width // 2
     lower = got_ref[:, :half]
-    upper = jnp.where(first_core(), got_ref[:, half:], traded_ref[0])
+    upper = jnp.where(first_core(), crossed_ref[...], traded_ref[0])
     rows = [block.reshape(modes * half, part) for block in (lower, upper)]
     coeffs = traded_ref[1].reshape(modes * half, 2 * count)
     back = dot3(coeffs.T, jnp.concatenate(rows, 1))
@@ -364,16 +359,17 @@
         buffers,
         FULL,
     )
-    crossed = kernel(share, struct(depth, half, part), (over_cores(first),))
+    first = over_cores(first)
+    crossed = kernel(share, struct(depth, half, part), (first,))
     crossed = cross(crossed, depth, modes)
     got = over_mode(kernel(bundle, struct(modes, width, part), (crossed, first, early)))
-    traded = over_cores(kernel(trade, struct(modes, half, part), (crossed, got)))
+    traded = over_cores(got[:, half:])
     resid, both = kernel(
-        remainder, (struct(count, part), struct(2 * few, part)), (got, traded, st_own)
-    )
+        remainder, (struct(count, part), struct(2 * few, part)), (got, crossed, traded, st_own)
+    )
+    own = kernel(join, struct(total, part), (got, crossed, traded))
     crossed = kernel(share_back, struct(depth, 1, used * part), (over_cores(both),))
     crossed = cross(crossed, depth, modes)
-    own = kernel(join, struct(total, part), (got, traded))
     rotated = dot(rotation[:total], own, 0, 0).reshape(modes, width, part)
     pieces = kernel(
         bundle_back, struct(modes, width + count, part), (crossed, rotated, resid)

time: 93.5 us -> 93.5 us (level)
    pallas_call x10 -> x9, Pallas kernels: 7.09 us -> 7.05 us  [kernel(): pl.pallas_call(body, out_shape=out, in_specs=specs or [VMEM] * len(args),...]
where the time goes in v9:
time: 93.5 us; the launch traced here: 92.9 us
  blocking collectives  67.1 us (72%)
  waiting for transfers between devices  8.28 us (9%)
  Pallas kernels  7.05 us (8%)
  starting transfers between devices  6.04 us (6%)
  matrix products  3.47 us (4%)
    all_to_all x2, blocking collectives, over_mode(): return lax.all_to_all(block, MODE, 0, 0, tiled=True)  30.3 us
    all_to_all x1, blocking collectives, cross(): lax.all_to_all(block, (Z, CORE) + MODE, 0, 0, tiled=True, axis_index_grou...  22.1 us
    all_gather x4, blocking collectives, over_cores(): return lax.all_gather(block, CORE, axis=0, tiled=False)  14.7 us
    all_to_all x1, waiting for transfers between devices, cross(): lax.all_to_all(block, (Z, CORE) + MODE, 0, 0, tiled=True, axis_index_grou...  8.28 us
    pallas_call x9, Pallas kernels, kernel(): pl.pallas_call(body, out_shape=out, in_specs=specs or [VMEM] * len(args),...  7.05 us
    all_to_all x1, starting transfers between devices, cross(): lax.all_to_all(block, (Z, CORE) + MODE, 0, 0, tiled=True, axis_index_grou...  6.04 us
    dot_general x1, matrix products, dot(): lax.dot_general(a, b, (((left,), (right,)), ((), ())), precision=HIGH)  3.47 us
  transfers between devices with their start and end apart: 1, of which 1 were waited for; matrix products, arithmetic and copies ran while one was open for 4% of the time, Pallas kernels for 0%

profile of v9, /device:TPU:1, one launch (start us, length us, event | category | flops | bytes accessed | tf_op | source)
XLA Modules:
  0.0 92.9 jit_solution(202373623828152415)
XLA Ops:
  0.6 1.9 %shard_map.50 = (f32[544,128]{1,0:T(8,128)S(1)}, f32[16,32,128]{2,1,0:T(8,128)S(1)}, f32[64,128]{1,0:T(8,128)S(1)}, f32[64,64]{1,0:T(8,128)S(1)}) custom-call(f32[64,2048]{1,0:T(8,128)} %bitcast.18, f32[64,2048]{1,0:T(8,128)} %bitcast.19, f32[1088,1024]{1,0:T(8,128)} %rot_ref.1), custom_call_target="tpu_custom_call" | custom-call | tf_op jit(solution)/shard_map/pallas_call | solution.py:297
  2.6 8.7 %all-gather = f32[1088,128]{1,0:T(8,128)S(1)} all-gather(f32[544,128]{1,0:T(8,128)S(1)} %get-tuple-element.10), channel_id=2, replica_groups=mesh['z'=16,'core'=2,'y'=4,'x'=4] {'core'}, dimensions={0}, use_global_device_ids=true | all-gather | bytes 835584 | tf_op jit(solution)/shard_map/all_gather | solution.py:324
  11.3 22.1 %all_to_all.20.crossed_ref = f32[16,32,128]{2,1,0:T(8,128)S(1)} all-to-all(f32[16,32,128]{2,1,0:T(8,128)S(1)} %shard_map.51), channel_id=1, replica_groups={{16,48,80,112,144,176,208,240,272,304,336,368,400,432,464,496},{17,49,8..., dimensions={0} | all-to-all | bytes 524288 | tf_op jit(solution)/shard_map/all_to_all | solution.py:318
  33.4 0.1 shard_map.52
  33.5 15.5 %all_to_all.21.got_ref = f32[16,64,128]{2,1,0:T(8,128)S(1)} all-to-all(f32[16,64,128]{2,1,0:T(8,128)S(1)} %shard_map.52), channel_id=1, replica_groups=mesh['z'=16,'core'=2,'y'=4,'x'=4] {'y','x'}, dimensions={0} | all-to-all | bytes 1048576 | tf_op jit(solution)/shard_map/all_to_all | solution.py:328
  49.1 2.2 %all-gather.1 = f32[32,32,128]{2,1,0:T(8,128)S(1)} all-gather(f32[16,32,128]{2,1,0:T(8,128)S(1)} %slice.8), channel_id=3, replica_groups=mesh['z'=16,'core'=2,'y'=4,'x'=4] {'core'}, dimensions={0}, use_global_device_ids=true | all-gather | bytes 786432 | tf_op jit(solution)/shard_map/all_gather | solution.py:324
  51.3 0.6 shard_map.53
  51.9 1.8 %all-gather.2 = f32[96,128]{1,0:T(8,128)S(1)} all-gather(f32[48,128]{1,0:T(8,128)S(1)} %get-tuple-element.13), channel_id=4, replica_groups=mesh['z'=16,'core'=2,'y'=4,'x'=4] {'core'}, dimensions={0}, use_global_device_ids=true | all-gather | bytes 73728 | tf_op jit(solution)/shard_map/all_gather | solution.py:324
  53.7 0.7 shard_map.54
  54.4 6.0 %all-to-all-start.2 = ((f32[16,1,2176]{2,1,0:T(1,128)}), f32[16,1,2176]{2,1,0:T(1,128)S(1)}, u32[]{:S(2)}, u32[]{:S(2)}) async-start(f32[16,1,2176]{2,1,0:T(1,128)} %shard_map.54), calls=%async_computation.2 | async-start | bytes 278528 | tf_op jit(solution)/shard_map/all_to_all | solution.py:318
  60.5 3.5 %fusion.2 = f32[1024,128]{0,1:T(8,128)S(1)} fusion(f32[1024,128]{1,0:T(8,128)S(1)} %shard_map.55, f32[1088,1024]{1,0:T(8,128)} %rot_ref.1), kind=kOutput, calls=%fused_computation.2 | convolution fusion | flops 805306368 | bytes 5242880 | tf_op jit(solution)/shard_map/dot_general | solution.py:28
  64.0 0.2 copy.6
  64.2 8.3 %all-to-all-done.2.crossed_ref = f32[16,1,2176]{2,1,0:T(1,128)S(1)} async-done(((f32[16,1,2176]{2,1,0:T(1,128)}), f32[16,1,2176]{2,1,0:T(1,128)S(1)}, u32[]{:S(2)}, u32[]{:S(2)}) %all-to-all-start.2) | async-done | bytes 139296 | tf_op jit(solution)/shard_map/all_to_all | solution.py:318
  72.5 0.1 shard_map.56
  72.6 14.7 %all_to_all.22.parts_ref = f32[16,128,128]{2,1,0:T(8,128)S(1)} all-to-all(f32[16,128,128]{2,1,0:T(8,128)S(1)} %shard_map.56), channel_id=1, replica_groups=mesh['z'=16,'core'=2,'y'=4,'x'=4] {'y','x'}, dimensions={0} | all-to-all | bytes 2097152 | tf_op jit(solution)/shard_map/all_to_all | solution.py:328
  87.3 2.0 %all-gather.3 = f32[34,1,2176]{2,1,0:T(1,128)S(1)} all-gather(f32[17,1,2176]{2,1,0:T(1,128)S(1)} %shard_map.57), channel_id=5, replica_groups=mesh['z'=16,'core'=2,'y'=4,'x'=4] {'core'}, dimensions={0}, use_global_device_ids=true | all-gather | bytes 443904 | tf_op jit(solution)/shard_map/all_gather | solution.py:324
  89.3 3.5 %shard_map.58 = (f32[64,2048]{1,0:T(8,128)}, f32[64,64]{1,0:T(8,128)}) custom-call(f32[2,17,1,2176]{3,2,1,0:T(1,128)S(1)} %bitcast.16, f32[64,64]{1,0:T(8,128)S(1)} %get-tuple-element.15.lower_cols_ref, f32[16,128,128]{2,1,0:T(8,128)S(1)} %all_to_all.22.parts_ref), custom_call_target="tpu_custom_call" | custom-call | tf_op jit(solution)/shard_map/pallas_call | solution.py:297
  (4 shorter events, 0.1 us)
Async XLA Ops:
  54.4 18.1 %all-to-all-start.2 = ((f32[16,1,2176]{2,1,0:T(1,128)}), f32[16,1,2176]{2,1,0:T(1,128)S(1)}, u32[]{:S(2)}, u32[]{:S(2)}) async-start(f32[16,1,2176]{2,1,0:T(1,128)} %shard_map.54), calls=%async_computation.2 | async-start | bytes 278528 | tf_op jit(solution)/shard_map/all_to_all | solution.py:318

commit v10 on v8

--- a/solution.py
+++ b/solution.py
@@ -89,6 +89,14 @@
     bt_ref, st_ref, rot_ref, first_ref, early_ref, own_ref, cols_ref, b_buf, s_buf, r_buf, sems
 ):
     step = b_buf.shape[1] // CHUNKS
+    place = lax.axis_index("y") * lax.axis_size("x") + lax.axis_index("x")
+    count, width = cols_ref.shape
+    wide = r_buf.shape[1]
+    side = pl.ds(pl.multiple_of(place // (wide // width) * wide, wide), wide)
+    columns = pltpu.make_async_copy(
+        rot_ref.at[pl.ds(rot_ref.shape[0] - count, count), side], r_buf, sems.at[2 * CHUNKS]
+    )
+    columns.start()
     copies = []
     for i in range(CHUNKS):
         cut = pl.ds(i * step, step)
@@ -98,14 +106,6 @@
             copies.append(copy)
     _, half, part = early_ref.shape
     each = step // part
-    place = lax.axis_index("y") * lax.axis_size("x") + lax.axis_index("x")
-    count, width = cols_ref.shape
-    wide = r_buf.shape[1]
-    side = pl.ds(pl.multiple_of(place // (wide // width) * wide, wide), wide)
-    columns = pltpu.make_async_copy(
-        rot_ref.at[pl.ds(rot_ref.shape[0] - count, count), side], r_buf, sems.at[2 * CHUNKS]
-    )
-    columns.start()
     total = None
     for i in range(CHUNKS):
         copies[2 * i].wait()

time: 93.5 us -> 93.5 us (level)
  no operation moved by 1% of the time
where the time goes in v10:
time: 93.5 us; the launch traced here: 92.9 us
  blocking collectives  67.1 us (72%)
  waiting for transfers between devices  8.28 us (9%)
  Pallas kernels  7.12 us (8%)
  starting transfers between devices  6.04 us (6%)
  matrix products  3.47 us (4%)
    all_to_all x2, blocking collectives, over_mode(): return lax.all_to_all(block, MODE, 0, 0, tiled=True)  30.3 us
    all_to_all x1, blocking collectives, cross(): lax.all_to_all(block, (Z, CORE) + MODE, 0, 0, tiled=True, axis_index_grou...  22.1 us
    all_gather x4, blocking collectives, over_cores(): return lax.all_gather(block, CORE, axis=0, tiled=False)  14.7 us
    all_to_all x1, waiting for transfers between devices, cross(): lax.all_to_all(block, (Z, CORE) + MODE, 0, 0, tiled=True, axis_index_grou...  8.28 us
    pallas_call x10, Pallas kernels, kernel(): pl.pallas_call(body, out_shape=out, in_specs=specs or [VMEM] * len(args),...  7.12 us
    all_to_all x1, starting transfers between devices, cross(): lax.all_to_all(block, (Z, CORE) + MODE, 0, 0, tiled=True, axis_index_grou...  6.04 us
    dot_general x1, matrix products, dot(): lax.dot_general(a, b, (((left,), (right,)), ((), ())), precision=HIGH)  3.47 us
  transfers between devices with their start and end apart: 1, of which 1 were waited for; matrix products, arithmetic and copies ran while one was open for 4% of the time, Pallas kernels for 0%

profile of v10, /device:TPU:1, one launch (start us, length us, event | category | flops | bytes accessed | tf_op | source)
XLA Modules:
  0.0 92.9 jit_solution(512653057291532233)
XLA Ops:
  0.6 2.0 %shard_map.50 = (f32[544,128]{1,0:T(8,128)S(1)}, f32[16,32,128]{2,1,0:T(8,128)S(1)}, f32[64,128]{1,0:T(8,128)S(1)}, f32[64,64]{1,0:T(8,128)S(1)}) custom-call(f32[64,2048]{1,0:T(8,128)} %bitcast.17, f32[64,2048]{1,0:T(8,128)} %bitcast.18, f32[1088,1024]{1,0:T(8,128)} %rot_ref.1), custom_call_target="tpu_custom_call" | custom-call | tf_op jit(solution)/shard_map/pallas_call | solution.py:302
  2.6 8.7 %all-gather = f32[1088,128]{1,0:T(8,128)S(1)} all-gather(f32[544,128]{1,0:T(8,128)S(1)} %get-tuple-element.10.first_ref), channel_id=2, replica_groups=mesh['z'=16,'core'=2,'y'=4,'x'=4] {'core'}, dimensions={0}, use_global_device_ids=true | all-gather | bytes 835584 | tf_op jit(solution)/shard_map/all_gather | solution.py:329
  11.4 22.1 %all_to_all.20.crossed_ref = f32[16,32,128]{2,1,0:T(8,128)S(1)} all-to-all(f32[16,32,128]{2,1,0:T(8,128)S(1)} %shard_map.51), channel_id=1, replica_groups={{16,48,80,112,144,176,208,240,272,304,336,368,400,432,464,496},{17,49,8..., dimensions={0} | all-to-all | bytes 524288 | tf_op jit(solution)/shard_map/all_to_all | solution.py:323
  33.5 0.1 shard_map.52
  33.5 15.5 %all_to_all.21.got_ref = f32[16,64,128]{2,1,0:T(8,128)S(1)} all-to-all(f32[16,64,128]{2,1,0:T(8,128)S(1)} %shard_map.52), channel_id=1, replica_groups=mesh['z'=16,'core'=2,'y'=4,'x'=4] {'y','x'}, dimensions={0} | all-to-all | bytes 1048576 | tf_op jit(solution)/shard_map/all_to_all | solution.py:333
  49.1 2.2 %all-gather.1 = f32[32,32,128]{2,1,0:T(8,128)S(1)} all-gather(f32[16,32,128]{2,1,0:T(8,128)S(1)} %shard_map.53), channel_id=3, replica_groups=mesh['z'=16,'core'=2,'y'=4,'x'=4] {'core'}, dimensions={0}, use_global_device_ids=true | all-gather | bytes 786432 | tf_op jit(solution)/shard_map/all_gather | solution.py:329
  51.3 0.6 shard_map.54
  51.9 1.8 %all-gather.2 = f32[96,128]{1,0:T(8,128)S(1)} all-gather(f32[48,128]{1,0:T(8,128)S(1)} %get-tuple-element.13), channel_id=4, replica_groups=mesh['z'=16,'core'=2,'y'=4,'x'=4] {'core'}, dimensions={0}, use_global_device_ids=true | all-gather | bytes 73728 | tf_op jit(solution)/shard_map/all_gather | solution.py:329
  53.8 0.7 shard_map.55
  54.5 6.0 %all-to-all-start.2 = ((f32[16,1,2176]{2,1,0:T(1,128)}), f32[16,1,2176]{2,1,0:T(1,128)S(1)}, u32[]{:S(2)}, u32[]{:S(2)}) async-start(f32[16,1,2176]{2,1,0:T(1,128)} %shard_map.55), calls=%async_computation.2 | async-start | bytes 278528 | tf_op jit(solution)/shard_map/all_to_all | solution.py:323
  60.6 3.5 %fusion.2 = f32[1024,128]{0,1:T(8,128)S(1)} fusion(f32[1024,128]{1,0:T(8,128)S(1)} %shard_map.56, f32[1088,1024]{1,0:T(8,128)} %rot_ref.1), kind=kOutput, calls=%fused_computation.2 | convolution fusion | flops 805306368 | bytes 5242880 | tf_op jit(solution)/shard_map/dot_general | solution.py:28
  64.0 0.2 copy.6
  64.2 8.3 %all-to-all-done.2.crossed_ref = f32[16,1,2176]{2,1,0:T(1,128)S(1)} async-done(((f32[16,1,2176]{2,1,0:T(1,128)}), f32[16,1,2176]{2,1,0:T(1,128)S(1)}, u32[]{:S(2)}, u32[]{:S(2)}) %all-to-all-start.2) | async-done | bytes 139296 | tf_op jit(solution)/shard_map/all_to_all | solution.py:323
  72.5 0.1 shard_map.57
  72.6 14.7 %all_to_all.22.parts_ref = f32[16,128,128]{2,1,0:T(8,128)S(1)} all-to-all(f32[16,128,128]{2,1,0:T(8,128)S(1)} %shard_map.57), channel_id=1, replica_groups=mesh['z'=16,'core'=2,'y'=4,'x'=4] {'y','x'}, dimensions={0} | all-to-all | bytes 2097152 | tf_op jit(solution)/shard_map/all_to_all | solution.py:333
  87.4 2.0 %all-gather.3 = f32[34,1,2176]{2,1,0:T(1,128)S(1)} all-gather(f32[17,1,2176]{2,1,0:T(1,128)S(1)} %shard_map.58), channel_id=5, replica_groups=mesh['z'=16,'core'=2,'y'=4,'x'=4] {'core'}, dimensions={0}, use_global_device_ids=true | all-gather | bytes 443904 | tf_op jit(solution)/shard_map/all_gather | solution.py:329
  89.4 3.5 %shard_map.59 = (f32[64,2048]{1,0:T(8,128)}, f32[64,64]{1,0:T(8,128)}) custom-call(f32[2,17,1,2176]{3,2,1,0:T(1,128)S(1)} %bitcast.15, f32[64,64]{1,0:T(8,128)S(1)} %get-tuple-element.15.lower_cols_ref, f32[16,128,128]{2,1,0:T(8,128)S(1)} %all_to_all.22.parts_ref), custom_call_target="tpu_custom_call" | custom-call | tf_op jit(solution)/shard_map/pallas_call | solution.py:302
  (4 shorter events, 0.2 us)
Async XLA Ops:
  54.5 18.1 %all-to-all-start.2 = ((f32[16,1,2176]{2,1,0:T(1,128)}), f32[16,1,2176]{2,1,0:T(1,128)S(1)}, u32[]{:S(2)}, u32[]{:S(2)}) async-start(f32[16,1,2176]{2,1,0:T(1,128)} %shard_map.55), calls=%async_computation.2 | async-start | bytes 278528 | tf_op jit(solution)/shard_map/all_to_all | solution.py:323
